TPU v7x, 128 devices: a whole 4x4x4 slice. The times are simulated.
128 devices in a mesh: tp: 8 (over z_hi, y), dec: 16 (over x, z_lo, core).
Axes of the slice: x: 4, y: 4, z: 4 (z_hi: 2, z_lo: 2; z = z_hi * 2 + z_lo), core: 2. Of those that a mesh axis runs over, the one named last changes fastest.
Arguments:
- queries: bfloat16 [16, 768, 8192], P('dec', None, 'tp'), may hold values from -30 to 30
- span_kv: bfloat16 [16, 768, 2048], P('dec', None, 'tp'), may hold values from -6 to 6
- page_pool: bfloat16 [1024, 128, 2048], P(('tp', 'dec')), may hold values from -6 to 6
- cache_slot: int32 [16, 128, 1], P('dec'), may hold values from 0 to 7
- cache_live: int32 [16, 128, 1], P('dec'), may hold values from 0 to 1, as said below
- span_dest: int32 [16, 6], P('dec'), may hold values from 0 to 15, as said below
Outputs:
- attn_out: bfloat16 [16, 768, 8192], P('dec', None, 'tp')
- decode_pages: bfloat16 [256, 128, 2048], P(('tp', 'dec'))
Inputs may be any that keep to these rules, and one draw needn't show every extreme that they name: `cache_slot`: entries with cache_live 0 are unused. Slots may be shared by several prompts. `cache_live`: each prompt has at most 32 live entries, and some prompt exactly 32; each prompt has some decode device with all 1 of its entries live. `span_dest`: the pages of one prompt go to distinct decode columns.
All inputs are finite; a program needn't handle non-finite values.
Results may differ from a plain program's by a relative error of at most 0.0028.
Values may be sent and summed in bfloat16 or wider, within the bound.
A program may use at most 128 MiB of HBM per device.

v0:
```python
import math

import jax
import jax.numpy as jnp
from jax import lax
from jax.sharding import PartitionSpec as P

HD = 128
PAGE = 128
CTXP = 32


def compact_slots(live_flags):
    flat_live = live_flags.reshape(-1)
    live_rank = jnp.cumsum(flat_live) - 1
    slot_ids = jnp.arange(flat_live.shape[0], dtype=jnp.int32)
    targets = jnp.arange(CTXP, dtype=jnp.int32)
    select_table = (flat_live[None, :] == 1) & (live_rank[None, :] == targets[:, None])
    live_index = jnp.sum(jnp.where(select_table, slot_ids[None, :], 0), axis=1)
    return (live_index, jnp.sum(flat_live))


def attend(query_block, kv_block, live_count, heads_query, group_size):
    span_rows = query_block.shape[0]
    total_keys = kv_block.shape[0]
    cached_keys = total_keys - span_rows
    score_scale = 1.0 / math.sqrt(HD)
    key_pos = jnp.arange(total_keys, dtype=jnp.int32)[None, :]
    query_pos = jnp.arange(span_rows, dtype=jnp.int32)[:, None]
    visible = jnp.where(
        key_pos < cached_keys, key_pos < live_count * PAGE, key_pos - cached_keys <= query_pos
    )

    def one_head(head_index):
        kv_head = head_index // group_size
        query_part = lax.dynamic_slice_in_dim(query_block, head_index * HD, HD, 1)
        key_part = lax.dynamic_slice_in_dim(kv_block, kv_head * 2 * HD, HD, 1)
        value_part = lax.dynamic_slice_in_dim(kv_block, kv_head * 2 * HD + HD, HD, 1)
        scores = (
            lax.dot_general(
                query_part, key_part, (((1,), (1,)), ((), ())), preferred_element_type=jnp.float32
            )
            * score_scale
        )
        scores = jnp.where(visible, scores, -jnp.inf)
        row_max = jnp.max(scores, axis=1, keepdims=True)
        weights = jnp.exp(scores - row_max)
        weight_total = jnp.sum(weights, axis=1, keepdims=True)
        mixed = jnp.dot(
            weights.astype(jnp.bfloat16), value_part, preferred_element_type=jnp.float32
        )
        return (mixed / weight_total).astype(jnp.bfloat16)

    heads_out = lax.map(one_head, jnp.arange(heads_query, dtype=jnp.int32))
    return jnp.transpose(heads_out, (1, 0, 2)).reshape(span_rows, heads_query * HD)


def body(queries, span_kv, page_pool, cache_slot, cache_live, span_dest):
    tp_size = lax.axis_size("tp")
    dec_size = lax.axis_size("dec")
    devices = tp_size * dec_size
    kv_width = span_kv.shape[2]
    slot_cap = cache_slot.shape[2]
    pool_slots = page_pool.shape[0]
    pool_view = page_pool.reshape(pool_slots, PAGE, tp_size, kv_width)
    source_rows = (jnp.arange(devices, dtype=jnp.int32) // dec_size)[:, None]
    requests = cache_slot[0]
    fetched = lax.all_to_all(
        pool_view[
            lax.all_to_all(requests, ("tp", "dec"), split_axis=0, concat_axis=0, tiled=True),
            :,
            source_rows,
        ],
        ("tp", "dec"),
        split_axis=0,
        concat_axis=0,
        tiled=True,
    ).reshape(devices * slot_cap, PAGE, kv_width)
    new_pages = span_kv[0].reshape(-1, PAGE, kv_width)
    chosen = (span_dest[0][None, :] == jnp.arange(dec_size, dtype=jnp.int32)[:, None]).astype(
        jnp.bfloat16
    )
    outgoing = jnp.einsum(
        "dp,pkc->dkc", chosen, new_pages, preferred_element_type=jnp.float32
    ).astype(jnp.bfloat16)
    placed = lax.all_to_all(
        lax.all_to_all(outgoing, "dec", split_axis=0, concat_axis=0, tiled=True),
        "tp",
        split_axis=0,
        concat_axis=2,
        tiled=True,
    )
    live_index, live_count = compact_slots(cache_live[0])
    cached = fetched[live_index]
    kv_block = jnp.concatenate([cached.reshape(-1, kv_width), span_kv[0]], axis=0)
    heads_query = queries.shape[2] // HD
    group_size = heads_query // (kv_width // (2 * HD))
    attn_out = attend(queries[0], kv_block, live_count, heads_query, group_size)[None]
    return (attn_out, placed)


def solution(mesh):
    in_specs = (
        P("dec", None, "tp"),
        P("dec", None, "tp"),
        P(("tp", "dec"), None, None),
        P("dec", None, None),
        P("dec", None, None),
        P("dec", None),
    )
    out_specs = (P("dec", None, "tp"), P(("tp", "dec"), None, None))
    return jax.shard_map(body, mesh=mesh, in_specs=in_specs, out_specs=out_specs, check_vma=False)
```

profile of v0, /device:TPU:19, one launch (start us, length us, event | category | flops | bytes accessed | tf_op | source)
XLA Modules:
  0.0 432.5 jit_solution(6915523950066352536)
XLA Ops:
  2.0 10.6 %all-to-all-start = ((s32[128,1,1]{2,1,0:T(1,128)}), s32[128,1,1]{2,1,0:T(1,128)S(1)}, u32[]{:S(2)}, u32[]{:S(2)}) async-start(s32[128,1,1]{2,1,0:T(1,128)} %copy.54), calls=%async_computation | async-start | bytes 131072 | tf_op jit(solution)/shard_map/all_to_all | solution.py:70
  19.6 18.9 %all_to_all.37 = bf16[16,128,256]{2,1,0:T(8,128)(2,1)} all-to-all(bf16[16,128,256]{2,1,0:T(8,128)(2,1)S(1)} %copy.64), channel_id=1, replica_groups=mesh['tp'=8,'dec'=16] {'dec'}, dimensions={0} | all-to-all | bytes 2097152 | tf_op jit(solution)/shard_map/all_to_all | solution.py:87
  43.7 6.4 %copy.53 = bf16[8,128,2048]{1,2,0:T(8,128)(2,1)} copy(bf16[8,128,2048]{2,1,0:T(8,128)(2,1)} %param.10) | data formatting | bytes 8388608 | tf_op args[2]
  50.1 6.5 %copy.59 = bf16[8,128,8,256]{3,1,2,0:T(8,128)(2,1)} copy(bf16[8,128,8,256]{1,3,2,0:T(8,128)(2,1)} %bitcast.41) | data formatting | bytes 8388608 | tf_op jit(solution)/shard_map/reshape | solution.py:65
  57.2 9.4 %gather_fusion = bf16[128,128,256]{2,1,0:T(8,128)(2,1)} fusion(bf16[8,128,8,256]{3,1,2,0:T(8,128)(2,1)} %copy.59, s32[128]{0:T(128)S(1)} %or_bitcast_fusion), kind=kCustom, calls=%fused_computation | custom fusion | bytes 16778240 | tf_op jit(solution)/shard_map/gather | solution.py:69
  66.6 10.0 %all-to-all-start.1 = ((bf16[128,1,128,256]{3,2,1,0:T(8,128)(2,1)}), bf16[128,1,128,256]{3,2,1,0:T(8,128)(2,1)}, u32[]{:S(2)}, u32[]{:S(2)}) async-start(bf16[128,1,128,256]{3,2,1,0:T(8,128)(2,1)} %bitcast.40), calls=%async_computation.1 | async-start | bytes 16777216 | tf_op jit(solution)/shard_map/all_to_all | solution.py:68
  79.6 115.6 %all-to-all-done.1 = bf16[128,1,128,256]{3,2,1,0:T(8,128)(2,1)} async-done(((bf16[128,1,128,256]{3,2,1,0:T(8,128)(2,1)}), bf16[128,1,128,256]{3,2,1,0:T(8,128)(2,1)}, u32[]{:S(2)}, u32[]{:S(2)}) %all-to-all-start.1) | async-done | bytes 8388640 | tf_op jit(solution)/shard_map/all_to_all | solution.py:68
  202.3 225.7 %while.13 = (s32[]{:T(128)}, bf16[8,768,128]{2,1,0:T(8,128)(2,1)}, s32[8]{0:T(128)S(1)}, bf16[768,1024]{1,0:T(8,128)(2,1)}, bf16[4864,256]{1,0:T(8,128)(2,1)S(1)...) while((s32[]{:T(128)}, bf16[8,768,128]{2,1,0:T(8,128)(2,1)}, ...), condition=%wide.region_6.7_spmd.clone, body=%wide.region_3.6_spmd.clone.sunk | while | flops 1946417664 | bytes 47759316 | solution.py:54
  206.5 8.6 %fusion.47 = (f32[768]{0:T(1024)S(1)}, f32[768,4864]{1,0:T(8,128)}) fusion(bf16[4864,256]{1,0:T(8,128)(2,1)S(1)} %get-tuple-element.215, s32[]{:T(128)S(6)} %select_n.117, bf16[768,1024]{1,0:T(8,128)(2,1)} %get-tuple-element.214, s32[]{:T(128)S(6)} %select_n.118, s32[4864]{0:T(1024)S(1)} %get-tuple-element.216, ...), kind=kOutput, calls=%fused_computation.46.clone.1 | convolution fusion | flops 974978304 | bytes 16417800 | tf_op jit(solution)/shard_map/while/body/eval_jaxpr/dot_general | solution.py:40
  215.1 7.3 %fusion.48 = f32[768]{0:T(1024)S(1)} fusion(f32[768,4864]{1,0:T(8,128)} %get-tuple-element.175, f32[768]{0:T(1024)S(1)} %get-tuple-element.176), kind=kLoop, calls=%fused_computation.7.clone.1 | loop fusion | flops 7470336 | bytes 14948352 | tf_op jit(solution)/shard_map/while/body/eval_jaxpr/reduce_sum | solution.py:48
  222.4 8.1 %fusion.49 = bf16[8,768,128]{2,1,0:T(8,128)(2,1)} fusion(bf16[8,768,128]{2,1,0:T(8,128)(2,1)} %get-tuple-element.195, s32[]{:T(128)} %get-tuple-element.194, bf16[4864,256]{1,0:T(8,128)(2,1)S(1)} %get-tuple-element.215, s32[]{:T(128)S(6)} %select_n.116, f32[768,4864]{1,0:T(8,128)} %get-tuple-element.175, f32[768]{0:T(1024)S(1)} %get-tuple-element.176, ...), kind=kOutput, calls=%fused_computation.16.clone.1 | convolution fusion | flops 963969024 | bytes 16392708 | tf_op jit(solution)/shard_map/while/body/eval_jaxpr/dot_general | solution.py:49
  234.7 8.6 %fusion.47 = (f32[768]{0:T(1024)S(1)}, f32[768,4864]{1,0:T(8,128)}) fusion(bf16[4864,256]{1,0:T(8,128)(2,1)S(1)} %get-tuple-element.215, s32[]{:T(128)S(6)} %select_n.117, bf16[768,1024]{1,0:T(8,128)(2,1)} %get-tuple-element.214, s32[]{:T(128)S(6)} %select_n.118, s32[4864]{0:T(1024)S(1)} %get-tuple-element.216, ...), kind=kOutput, calls=%fused_computation.46.clone.1 | convolution fusion | flops 974978304 | bytes 16417800 | tf_op jit(solution)/shard_map/while/body/eval_jaxpr/dot_general | solution.py:40
  243.3 7.3 %fusion.48 = f32[768]{0:T(1024)S(1)} fusion(f32[768,4864]{1,0:T(8,128)} %get-tuple-element.175, f32[768]{0:T(1024)S(1)} %get-tuple-element.176), kind=kLoop, calls=%fused_computation.7.clone.1 | loop fusion | flops 7470336 | bytes 14948352 | tf_op jit(solution)/shard_map/while/body/eval_jaxpr/reduce_sum | solution.py:48
  250.6 8.1 %fusion.49 = bf16[8,768,128]{2,1,0:T(8,128)(2,1)} fusion(bf16[8,768,128]{2,1,0:T(8,128)(2,1)} %get-tuple-element.195, s32[]{:T(128)} %get-tuple-element.194, bf16[4864,256]{1,0:T(8,128)(2,1)S(1)} %get-tuple-element.215, s32[]{:T(128)S(6)} %select_n.116, f32[768,4864]{1,0:T(8,128)} %get-tuple-element.175, f32[768]{0:T(1024)S(1)} %get-tuple-element.176, ...), kind=kOutput, calls=%fused_computation.16.clone.1 | convolution fusion | flops 963969024 | bytes 16392708 | tf_op jit(solution)/shard_map/while/body/eval_jaxpr/dot_general | solution.py:49
  262.9 8.6 %fusion.47 = (f32[768]{0:T(1024)S(1)}, f32[768,4864]{1,0:T(8,128)}) fusion(bf16[4864,256]{1,0:T(8,128)(2,1)S(1)} %get-tuple-element.215, s32[]{:T(128)S(6)} %select_n.117, bf16[768,1024]{1,0:T(8,128)(2,1)} %get-tuple-element.214, s32[]{:T(128)S(6)} %select_n.118, s32[4864]{0:T(1024)S(1)} %get-tuple-element.216, ...), kind=kOutput, calls=%fused_computation.46.clone.1 | convolution fusion | flops 974978304 | bytes 16417800 | tf_op jit(solution)/shard_map/while/body/eval_jaxpr/dot_general | solution.py:40
  271.5 7.3 %fusion.48 = f32[768]{0:T(1024)S(1)} fusion(f32[768,4864]{1,0:T(8,128)} %get-tuple-element.175, f32[768]{0:T(1024)S(1)} %get-tuple-element.176), kind=kLoop, calls=%fused_computation.7.clone.1 | loop fusion | flops 7470336 | bytes 14948352 | tf_op jit(solution)/shard_map/while/body/eval_jaxpr/reduce_sum | solution.py:48
  278.9 8.1 %fusion.49 = bf16[8,768,128]{2,1,0:T(8,128)(2,1)} fusion(bf16[8,768,128]{2,1,0:T(8,128)(2,1)} %get-tuple-element.195, s32[]{:T(128)} %get-tuple-element.194, bf16[4864,256]{1,0:T(8,128)(2,1)S(1)} %get-tuple-element.215, s32[]{:T(128)S(6)} %select_n.116, f32[768,4864]{1,0:T(8,128)} %get-tuple-element.175, f32[768]{0:T(1024)S(1)} %get-tuple-element.176, ...), kind=kOutput, calls=%fused_computation.16.clone.1 | convolution fusion | flops 963969024 | bytes 16392708 | tf_op jit(solution)/shard_map/while/body/eval_jaxpr/dot_general | solution.py:49
  291.1 8.6 %fusion.47 = (f32[768]{0:T(1024)S(1)}, f32[768,4864]{1,0:T(8,128)}) fusion(bf16[4864,256]{1,0:T(8,128)(2,1)S(1)} %get-tuple-element.215, s32[]{:T(128)S(6)} %select_n.117, bf16[768,1024]{1,0:T(8,128)(2,1)} %get-tuple-element.214, s32[]{:T(128)S(6)} %select_n.118, s32[4864]{0:T(1024)S(1)} %get-tuple-element.216, ...), kind=kOutput, calls=%fused_computation.46.clone.1 | convolution fusion | flops 974978304 | bytes 16417800 | tf_op jit(solution)/shard_map/while/body/eval_jaxpr/dot_general | solution.py:40
  299.7 7.3 %fusion.48 = f32[768]{0:T(1024)S(1)} fusion(f32[768,4864]{1,0:T(8,128)} %get-tuple-element.175, f32[768]{0:T(1024)S(1)} %get-tuple-element.176), kind=kLoop, calls=%fused_computation.7.clone.1 | loop fusion | flops 7470336 | bytes 14948352 | tf_op jit(solution)/shard_map/while/body/eval_jaxpr/reduce_sum | solution.py:48
  307.1 8.1 %fusion.49 = bf16[8,768,128]{2,1,0:T(8,128)(2,1)} fusion(bf16[8,768,128]{2,1,0:T(8,128)(2,1)} %get-tuple-element.195, s32[]{:T(128)} %get-tuple-element.194, bf16[4864,256]{1,0:T(8,128)(2,1)S(1)} %get-tuple-element.215, s32[]{:T(128)S(6)} %select_n.116, f32[768,4864]{1,0:T(8,128)} %get-tuple-element.175, f32[768]{0:T(1024)S(1)} %get-tuple-element.176, ...), kind=kOutput, calls=%fused_computation.16.clone.1 | convolution fusion | flops 963969024 | bytes 16392708 | tf_op jit(solution)/shard_map/while/body/eval_jaxpr/dot_general | solution.py:49
  319.3 8.6 %fusion.47 = (f32[768]{0:T(1024)S(1)}, f32[768,4864]{1,0:T(8,128)}) fusion(bf16[4864,256]{1,0:T(8,128)(2,1)S(1)} %get-tuple-element.215, s32[]{:T(128)S(6)} %select_n.117, bf16[768,1024]{1,0:T(8,128)(2,1)} %get-tuple-element.214, s32[]{:T(128)S(6)} %select_n.118, s32[4864]{0:T(1024)S(1)} %get-tuple-element.216, ...), kind=kOutput, calls=%fused_computation.46.clone.1 | convolution fusion | flops 974978304 | bytes 16417800 | tf_op jit(solution)/shard_map/while/body/eval_jaxpr/dot_general | solution.py:40
  327.9 7.3 %fusion.48 = f32[768]{0:T(1024)S(1)} fusion(f32[768,4864]{1,0:T(8,128)} %get-tuple-element.175, f32[768]{0:T(1024)S(1)} %get-tuple-element.176), kind=kLoop, calls=%fused_computation.7.clone.1 | loop fusion | flops 7470336 | bytes 14948352 | tf_op jit(solution)/shard_map/while/body/eval_jaxpr/reduce_sum | solution.py:48
  335.3 8.1 %fusion.49 = bf16[8,768,128]{2,1,0:T(8,128)(2,1)} fusion(bf16[8,768,128]{2,1,0:T(8,128)(2,1)} %get-tuple-element.195, s32[]{:T(128)} %get-tuple-element.194, bf16[4864,256]{1,0:T(8,128)(2,1)S(1)} %get-tuple-element.215, s32[]{:T(128)S(6)} %select_n.116, f32[768,4864]{1,0:T(8,128)} %get-tuple-element.175, f32[768]{0:T(1024)S(1)} %get-tuple-element.176, ...), kind=kOutput, calls=%fused_computation.16.clone.1 | convolution fusion | flops 963969024 | bytes 16392708 | tf_op jit(solution)/shard_map/while/body/eval_jaxpr/dot_general | solution.py:49
  347.5 8.6 %fusion.47 = (f32[768]{0:T(1024)S(1)}, f32[768,4864]{1,0:T(8,128)}) fusion(bf16[4864,256]{1,0:T(8,128)(2,1)S(1)} %get-tuple-element.215, s32[]{:T(128)S(6)} %select_n.117, bf16[768,1024]{1,0:T(8,128)(2,1)} %get-tuple-element.214, s32[]{:T(128)S(6)} %select_n.118, s32[4864]{0:T(1024)S(1)} %get-tuple-element.216, ...), kind=kOutput, calls=%fused_computation.46.clone.1 | convolution fusion | flops 974978304 | bytes 16417800 | tf_op jit(solution)/shard_map/while/body/eval_jaxpr/dot_general | solution.py:40
  356.1 7.3 %fusion.48 = f32[768]{0:T(1024)S(1)} fusion(f32[768,4864]{1,0:T(8,128)} %get-tuple-element.175, f32[768]{0:T(1024)S(1)} %get-tuple-element.176), kind=kLoop, calls=%fused_computation.7.clone.1 | loop fusion | flops 7470336 | bytes 14948352 | tf_op jit(solution)/shard_map/while/body/eval_jaxpr/reduce_sum | solution.py:48
  363.5 8.1 %fusion.49 = bf16[8,768,128]{2,1,0:T(8,128)(2,1)} fusion(bf16[8,768,128]{2,1,0:T(8,128)(2,1)} %get-tuple-element.195, s32[]{:T(128)} %get-tuple-element.194, bf16[4864,256]{1,0:T(8,128)(2,1)S(1)} %get-tuple-element.215, s32[]{:T(128)S(6)} %select_n.116, f32[768,4864]{1,0:T(8,128)} %get-tuple-element.175, f32[768]{0:T(1024)S(1)} %get-tuple-element.176, ...), kind=kOutput, calls=%fused_computation.16.clone.1 | convolution fusion | flops 963969024 | bytes 16392708 | tf_op jit(solution)/shard_map/while/body/eval_jaxpr/dot_general | solution.py:49
  375.7 8.6 %fusion.47 = (f32[768]{0:T(1024)S(1)}, f32[768,4864]{1,0:T(8,128)}) fusion(bf16[4864,256]{1,0:T(8,128)(2,1)S(1)} %get-tuple-element.215, s32[]{:T(128)S(6)} %select_n.117, bf16[768,1024]{1,0:T(8,128)(2,1)} %get-tuple-element.214, s32[]{:T(128)S(6)} %select_n.118, s32[4864]{0:T(1024)S(1)} %get-tuple-element.216, ...), kind=kOutput, calls=%fused_computation.46.clone.1 | convolution fusion | flops 974978304 | bytes 16417800 | tf_op jit(solution)/shard_map/while/body/eval_jaxpr/dot_general | solution.py:40
  384.4 7.3 %fusion.48 = f32[768]{0:T(1024)S(1)} fusion(f32[768,4864]{1,0:T(8,128)} %get-tuple-element.175, f32[768]{0:T(1024)S(1)} %get-tuple-element.176), kind=kLoop, calls=%fused_computation.7.clone.1 | loop fusion | flops 7470336 | bytes 14948352 | tf_op jit(solution)/shard_map/while/body/eval_jaxpr/reduce_sum | solution.py:48
  391.7 8.1 %fusion.49 = bf16[8,768,128]{2,1,0:T(8,128)(2,1)} fusion(bf16[8,768,128]{2,1,0:T(8,128)(2,1)} %get-tuple-element.195, s32[]{:T(128)} %get-tuple-element.194, bf16[4864,256]{1,0:T(8,128)(2,1)S(1)} %get-tuple-element.215, s32[]{:T(128)S(6)} %select_n.116, f32[768,4864]{1,0:T(8,128)} %get-tuple-element.175, f32[768]{0:T(1024)S(1)} %get-tuple-element.176, ...), kind=kOutput, calls=%fused_computation.16.clone.1 | convolution fusion | flops 963969024 | bytes 16392708 | tf_op jit(solution)/shard_map/while/body/eval_jaxpr/dot_general | solution.py:49
  403.9 8.6 %fusion.47 = (f32[768]{0:T(1024)S(1)}, f32[768,4864]{1,0:T(8,128)}) fusion(bf16[4864,256]{1,0:T(8,128)(2,1)S(1)} %get-tuple-element.215, s32[]{:T(128)S(6)} %select_n.117, bf16[768,1024]{1,0:T(8,128)(2,1)} %get-tuple-element.214, s32[]{:T(128)S(6)} %select_n.118, s32[4864]{0:T(1024)S(1)} %get-tuple-element.216, ...), kind=kOutput, calls=%fused_computation.46.clone.1 | convolution fusion | flops 974978304 | bytes 16417800 | tf_op jit(solution)/shard_map/while/body/eval_jaxpr/dot_general | solution.py:40
  412.6 7.3 %fusion.48 = f32[768]{0:T(1024)S(1)} fusion(f32[768,4864]{1,0:T(8,128)} %get-tuple-element.175, f32[768]{0:T(1024)S(1)} %get-tuple-element.176), kind=kLoop, calls=%fused_computation.7.clone.1 | loop fusion | flops 7470336 | bytes 14948352 | tf_op jit(solution)/shard_map/while/body/eval_jaxpr/reduce_sum | solution.py:48
  419.9 8.1 %fusion.49 = bf16[8,768,128]{2,1,0:T(8,128)(2,1)} fusion(bf16[8,768,128]{2,1,0:T(8,128)(2,1)} %get-tuple-element.195, s32[]{:T(128)} %get-tuple-element.194, bf16[4864,256]{1,0:T(8,128)(2,1)S(1)} %get-tuple-element.215, s32[]{:T(128)S(6)} %select_n.116, f32[768,4864]{1,0:T(8,128)} %get-tuple-element.175, f32[768]{0:T(1024)S(1)} %get-tuple-element.176, ...), kind=kOutput, calls=%fused_computation.16.clone.1 | convolution fusion | flops 963969024 | bytes 16392708 | tf_op jit(solution)/shard_map/while/body/eval_jaxpr/dot_general | solution.py:49
  (46 shorter events, 33.3 us)
Async XLA Ops:
  2.0 17.6 %all-to-all-start = ((s32[128,1,1]{2,1,0:T(1,128)}), s32[128,1,1]{2,1,0:T(1,128)S(1)}, u32[]{:S(2)}, u32[]{:S(2)}) async-start(s32[128,1,1]{2,1,0:T(1,128)} %copy.54), calls=%async_computation | async-start | bytes 131072 | tf_op jit(solution)/shard_map/all_to_all | solution.py:70
  38.5 28.1 %all-to-all-start.3 = ((bf16[16,128,256]{2,1,0:T(8,128)(2,1)}), bf16[16,128,256]{2,1,0:T(8,128)(2,1)S(1)}, u32[]{:S(2)}, u32[]{:S(2)}) async-start(bf16[16,128,256]{2,1,0:T(8,128)(2,1)} %all_to_all.37), calls=%async_computation.3 | async-start | bytes 2097152 | tf_op jit(solution)/shard_map/all_to_all | solution.py:86
  66.6 10.0 %copy-start.1 = (s32[1,128,1]{1,2,0:T(1,128)S(1)}, s32[1,128,1]{1,2,0:T(1,128)}, u32[]{:S(2)}) copy-start(s32[1,128,1]{1,2,0:T(1,128)} %param.12) | copy-start | bytes 1540
  66.6 128.5 %all-to-all-start.1 = ((bf16[128,1,128,256]{3,2,1,0:T(8,128)(2,1)}), bf16[128,1,128,256]{3,2,1,0:T(8,128)(2,1)}, u32[]{:S(2)}, u32[]{:S(2)}) async-start(bf16[128,1,128,256]{3,2,1,0:T(8,128)(2,1)} %bitcast.40), calls=%async_computation.1 | async-start | bytes 16777216 | tf_op jit(solution)/shard_map/all_to_all | solution.py:68
  76.6 124.0 %copy-start = (bf16[1,768,256]{2,1,0:T(8,128)(2,1)S(1)}, bf16[1,768,256]{2,1,0:T(8,128)(2,1)}, u32[]{:S(2)}) copy-start(bf16[1,768,256]{2,1,0:T(8,128)(2,1)} %param.9) | copy-start | bytes 1179652
where the time goes:
time: 434 us; the launch traced here: 432 us
  matrix products  135 us (31%)
  waiting for transfers between devices  121 us (28%)
  other arithmetic  61.7 us (14%)
  local copies, waits for them, and re-layouts  40.7 us (9%)
  loops' own time  27.9 us (6%)
  starting transfers between devices  25.8 us (6%)
  blocking collectives  18.9 us (4%)
    all_to_all x1, waiting for transfers between devices, body(): lax.all_to_all(pool_view[lax.all_to_all(requests, ('tp', 'dec'), split_ax...  116 us
    dot_general x8, matrix products, one_head(): lax.dot_general(query_part, key_part, (((1,), (1,)), ((), ())), preferred...  69 us
    dot_general x8, matrix products, one_head(): jnp.dot(weights.astype(jnp.bfloat16), value_part, preferred_element_type=...  64.8 us
    reduce_sum x8, other arithmetic, one_head(): weight_total = jnp.sum(weights, axis=1, keepdims=True)  58.7 us
    another operation x1, loops' own time, attend(): heads_out = lax.map(one_head, jnp.arange(heads_query, dtype=jnp.int32))  27.9 us
    all_to_all x1, blocking collectives, body(): lax.all_to_all(outgoing, 'dec', split_axis=0, concat_axis=0, tiled=True)  18.9 us
    all_to_all x1, starting transfers between devices, body(): lax.all_to_all(requests, ('tp', 'dec'), split_axis=0, concat_axis=0, tile...  10.6 us
    all_to_all x1, starting transfers between devices, body(): lax.all_to_all(pool_view[lax.all_to_all(requests, ('tp', 'dec'), split_ax...  9.97 us
  transfers between devices with their start and end apart: 3, of which 2 were waited for; matrix products, arithmetic and copies ran while one was open for 6% of the time, Pallas kernels for 0%

commit v1 on v0

v1 whole, which is shorter than its diff:
```python
import functools
import math

import jax
import jax.numpy as jnp
from jax import lax
from jax.experimental import pallas as pl
from jax.experimental.pallas import tpu as pltpu
from jax.sharding import PartitionSpec as P

HD = 128
PAGE = 128
CTXP = 32
QT = 256
KC = 512
LOG2E = 1.4426950408889634
NEG = -1e30


def compact_slots(live_flags):
    flat_live = live_flags.reshape(-1)
    live_rank = jnp.cumsum(flat_live) - 1
    slot_ids = jnp.arange(flat_live.shape[0], dtype=jnp.int32)
    targets = jnp.arange(CTXP, dtype=jnp.int32)
    select_table = (flat_live[None, :] == 1) & (live_rank[None, :] == targets[:, None])
    live_index = jnp.sum(jnp.where(select_table, slot_ids[None, :], 0), axis=1)
    return (live_index, jnp.sum(flat_live))


def attend_kernel(
    heads, span, index_ref, count_ref, q_ref, span_ref, pages_ref, out_ref, k_ref, v_ref, s_ref, mx_ref, acc_ref, sem
):
    cached = CTXP * PAGE
    tiles = span // QT
    coef = LOG2E / math.sqrt(HD)

    def page_copies(p):
        src = pages_ref.at[index_ref[p]]
        rows = pl.ds(pl.multiple_of(p * PAGE, PAGE), PAGE)
        return (
            pltpu.make_async_copy(src.at[:, pl.ds(0, HD)], k_ref.at[rows], sem.at[0, p]),
            pltpu.make_async_copy(src.at[:, pl.ds(HD, HD)], v_ref.at[rows, pl.ds(0, HD)], sem.at[1, p]),
        )

    @pl.loop(0, CTXP)
    def _(p):
        for copy in page_copies(p):
            copy.start()

    v_ref[:, HD:] = jnp.ones((cached + span, HD), jnp.bfloat16)
    k_ref[cached:, :] = span_ref[:, :HD]
    v_ref[cached:, :HD] = span_ref[:, HD:]

    @pl.loop(0, CTXP)
    def _(p):
        for copy in page_copies(p):
            copy.wait()

    live = count_ref[0]
    full = live // (KC // PAGE)
    rest = live - full * (KC // PAGE)

    def q_tile(h, i):
        return q_ref[pl.ds(i * QT, QT), pl.ds(pl.multiple_of(h * HD, HD), HD)]

    def fold(part, width):
        out = part[:, :HD]
        for c in range(1, width // HD):
            out = jnp.maximum(out, part[:, c * HD : (c + 1) * HD])
        return out

    def score(slot, q, start, width, mask=None):
        part = lax.dot_general(
            q, k_ref[pl.ds(start, width), :], (((1,), (1,)), ((), ())), preferred_element_type=jnp.float32
        )
        if mask is not None:
            part = jnp.where(mask, part, NEG)
        s_ref[slot, :, pl.ds(start, width)] = part
        mx_ref[slot] = jnp.maximum(mx_ref[slot], fold(part, width))

    def mix(slot, top, start, width):
        part = s_ref[slot, :, pl.ds(start, width)]
        weights = [
            jnp.exp2((part[:, c * HD : (c + 1) * HD] - top) * coef).astype(jnp.bfloat16) for c in range(width // HD)
        ]
        acc_ref[...] += jnp.dot(
            jnp.concatenate(weights, axis=1), v_ref[pl.ds(start, width), :], preferred_element_type=jnp.float32
        )

    def rest_mask():
        return lax.broadcasted_iota(jnp.int32, (QT, KC), 1) < rest * PAGE

    def diagonal_mask():
        return lax.broadcasted_iota(jnp.int32, (QT, QT), 1) <= lax.broadcasted_iota(jnp.int32, (QT, QT), 0)

    def step(score_of, mix_of):
        if score_of is not None:
            sh, si, ss = score_of
            q = q_tile(sh, si)
            mx_ref[ss] = jnp.full((QT, HD), NEG, jnp.float32)
        if mix_of is not None:
            mh, mi, ms = mix_of
            top = jnp.broadcast_to(jnp.max(mx_ref[ms], axis=1, keepdims=True), (QT, HD))
            acc_ref[...] = jnp.zeros_like(acc_ref)

        @pl.loop(0, full)
        def _(j):
            start = pl.multiple_of(j * KC, KC)
            if score_of is not None:
                score(ss, q, start, KC)
            if mix_of is not None:
                mix(ms, top, start, KC)

        @pl.when(rest > 0)
        def _():
            start = pl.multiple_of(full * KC, KC)
            if score_of is not None:
                score(ss, q, start, KC, rest_mask())
            if mix_of is not None:
                mix(ms, top, start, KC)

        if score_of is not None:
            for b in range(si):
                score(ss, q, cached + b * QT, QT)
            score(ss, q, cached + si * QT, QT, diagonal_mask())
        if mix_of is not None:
            mix(ms, top, cached, (mi + 1) * QT)
            acc = acc_ref[...]
            out_ref[pl.ds(mi * QT, QT), pl.ds(pl.multiple_of(mh * HD, HD), HD)] = (
                acc[:, :HD] / acc[:, HD:]
            ).astype(out_ref.dtype)

    step((0, 0, 0), None)

    @pl.loop(0, heads // 2)
    def _(hh):
        for n in range(2 * tiles):
            now = (hh * 2 + n // tiles, n % tiles, n % 2)
            m = n + 1
            later = (jnp.minimum(hh * 2 + m // tiles, heads - 1), m % tiles, m % 2)
            step(later, now)


def attend(queries, span_kv, pages, live_index, live_count):
    span, width = queries.shape
    heads = width // HD
    cached = CTXP * PAGE
    vmem = pl.BlockSpec(memory_space=pltpu.VMEM)
    smem = pl.BlockSpec(memory_space=pltpu.SMEM)
    return pl.pallas_call(
        functools.partial(attend_kernel, heads, span),
        out_shape=jax.ShapeDtypeStruct((span, width), jnp.bfloat16),
        in_specs=[smem, smem, vmem, vmem, pl.BlockSpec(memory_space=pl.ANY)],
        out_specs=vmem,
        scratch_shapes=[
            pltpu.VMEM((cached + span, HD), jnp.bfloat16),
            pltpu.VMEM((cached + span, 2 * HD), jnp.bfloat16),
            pltpu.VMEM((2, QT, cached + span), jnp.float32),
            pltpu.VMEM((2, QT, HD), jnp.float32),
            pltpu.VMEM((QT, 2 * HD), jnp.float32),
            pltpu.SemaphoreType.DMA((2, CTXP)),
        ],
        compiler_params=pltpu.CompilerParams(vmem_limit_bytes=48 * 1024 * 1024),
        cost_estimate=pl.CostEstimate(
            flops=4 * span * width * cached, bytes_accessed=8 * 1024 * 1024, transcendentals=span * heads * cached
        ),
    )(live_index, live_count, queries, span_kv, pages)


def body(queries, span_kv, page_pool, cache_slot, cache_live, span_dest):
    tp_size = lax.axis_size("tp")
    dec_size = lax.axis_size("dec")
    devices = tp_size * dec_size
    kv_width = span_kv.shape[2]
    pool_slots = page_pool.shape[0]
    pool_view = page_pool.reshape(pool_slots, PAGE, tp_size, kv_width)
    source_rows = (jnp.arange(devices, dtype=jnp.int32) // dec_size)[:, None]
    requests = cache_slot[0]
    fetched = lax.all_to_all(
        pool_view[
            lax.all_to_all(requests, ("tp", "dec"), split_axis=0, concat_axis=0, tiled=True),
            :,
            source_rows,
        ],
        ("tp", "dec"),
        split_axis=0,
        concat_axis=0,
        tiled=True,
    ).reshape(devices, PAGE, kv_width)
    new_pages = span_kv[0].reshape(-1, PAGE, kv_width)
    chosen = (span_dest[0][None, :] == jnp.arange(dec_size, dtype=jnp.int32)[:, None]).astype(
        jnp.bfloat16
    )
    outgoing = jnp.einsum(
        "dp,pkc->dkc", chosen, new_pages, preferred_element_type=jnp.float32
    ).astype(jnp.bfloat16)
    placed = lax.all_to_all(
        lax.all_to_all(outgoing, "dec", split_axis=0, concat_axis=0, tiled=True),
        "tp",
        split_axis=0,
        concat_axis=2,
        tiled=True,
    )
    live_index, live_count = compact_slots(cache_live[0])
    attn_out = attend(queries[0], span_kv[0], fetched, live_index, live_count.reshape(1))[None]
    return (attn_out, placed)


def solution(mesh):
    in_specs = (
        P("dec", None, "tp"),
        P("dec", None, "tp"),
        P(("tp", "dec"), None, None),
        P("dec", None, None),
        P("dec", None, None),
        P("dec", None),
    )
    out_specs = (P("dec", None, "tp"), P(("tp", "dec"), None, None))
    return jax.shard_map(body, mesh=mesh, in_specs=in_specs, out_specs=out_specs, check_vma=False)
```

time: 434 us -> 273 us (0.63)
  the two profiles are of different devices: /device:TPU:19 before, /device:TPU:12 now
where the time goes in v1:
time: 273 us; the launch traced here: 272 us
  waiting for transfers between devices  122 us (45%)
  Pallas kernels  76.4 us (28%)
  local copies, waits for them, and re-layouts  25.5 us (9%)
  starting transfers between devices  25 us (9%)
  blocking collectives  19.2 us (7%)
    all_to_all x1, waiting for transfers between devices, body(): lax.all_to_all(pool_view[lax.all_to_all(requests, ('tp', 'dec'), split_ax...  117 us
    pallas_call x1, Pallas kernels, attend(): pl.pallas_call(functools.partial(attend_kernel, heads, span), out_shape=j...  76.4 us
    all_to_all x1, blocking collectives, body(): lax.all_to_all(outgoing, 'dec', split_axis=0, concat_axis=0, tiled=True)  19.2 us
    all_to_all x1, starting transfers between devices, body(): lax.all_to_all(requests, ('tp', 'dec'), split_axis=0, concat_axis=0, tile...  10.4 us
    all_to_all x1, starting transfers between devices, body(): lax.all_to_all(pool_view[lax.all_to_all(requests, ('tp', 'dec'), split_ax...  9.67 us
    gather x1, local copies, waits for them, and re-layouts, body(): pool_view[lax.all_to_all(requests, ('tp', 'dec'), split_axis=0, concat_ax...  9.39 us
    reshape x1, local copies, waits for them, and re-layouts, body(): pool_view = page_pool.reshape(pool_slots, PAGE, tp_size, kv_width)  6.47 us
    unnamed x7, local copies, waits for them, and re-layouts  6.45 us
  transfers between devices with their start and end apart: 3, of which 2 were waited for; matrix products, arithmetic and copies ran while one was open for 10% of the time, Pallas kernels for 0%

profile of v1, /device:TPU:12, one launch (start us, length us, event | category | flops | bytes accessed | tf_op | source)
XLA Modules:
  0.0 272.2 jit_solution(1853309909348130071)
XLA Ops:
  0.6 1.4 copy.49
  2.0 10.4 %all-to-all-start = ((s32[128,1,1]{2,1,0:T(1,128)}), s32[128,1,1]{2,1,0:T(1,128)S(1)}, u32[]{:S(2)}, u32[]{:S(2)}) async-start(s32[128,1,1]{2,1,0:T(1,128)} %copy.49), calls=%async_computation | async-start | bytes 131072 | tf_op jit(solution)/shard_map/all_to_all | solution.py:181
  12.4 1.6 convolution_convert_fusion
  14.0 0.3 copy.57
  14.4 5.3 %all-to-all-done = s32[128,1,1]{2,1,0:T(1,128)S(1)} async-done(((s32[128,1,1]{2,1,0:T(1,128)}), s32[128,1,1]{2,1,0:T(1,128)S(1)}, u32[]{:S(2)}, u32[]{:S(2)}) %all-to-all-start) | async-done | bytes 544 | tf_op jit(solution)/shard_map/all_to_all | solution.py:181
  19.7 19.2 %all_to_all.37 = bf16[16,128,256]{2,1,0:T(8,128)(2,1)} all-to-all(bf16[16,128,256]{2,1,0:T(8,128)(2,1)S(1)} %copy.57), channel_id=1, replica_groups=mesh['tp'=8,'dec'=16] {'dec'}, dimensions={0} | all-to-all | bytes 2097152 | tf_op jit(solution)/shard_map/all_to_all | solution.py:198
  38.8 4.9 %all-to-all-start.3 = ((bf16[16,128,256]{2,1,0:T(8,128)(2,1)}), bf16[16,128,256]{2,1,0:T(8,128)(2,1)S(1)}, u32[]{:S(2)}, u32[]{:S(2)}) async-start(bf16[16,128,256]{2,1,0:T(8,128)(2,1)} %all_to_all.37), calls=%async_computation.3 | async-start | bytes 2097152 | tf_op jit(solution)/shard_map/all_to_all | solution.py:197
  43.8 6.4 %copy.48 = bf16[8,128,2048]{1,2,0:T(8,128)(2,1)} copy(bf16[8,128,2048]{2,1,0:T(8,128)(2,1)} %param.8) | data formatting | bytes 8388608 | tf_op args[2]
  50.2 6.5 %copy.54 = bf16[8,128,8,256]{3,1,2,0:T(8,128)(2,1)} copy(bf16[8,128,8,256]{1,3,2,0:T(8,128)(2,1)} %bitcast.31) | data formatting | bytes 8388608 | tf_op jit(solution)/shard_map/reshape | solution.py:176
  56.7 0.1 copy.50
  56.9 0.1 copy.51
  56.9 0.1 and_select_fusion
  57.0 0.1 copy.52
  57.0 0.1 compare_select_fusion
  57.1 0.1 copy.53
  57.2 9.4 %gather_fusion = bf16[128,128,256]{2,1,0:T(8,128)(2,1)} fusion(bf16[8,128,8,256]{3,1,2,0:T(8,128)(2,1)} %copy.54, s32[128]{0:T(128)S(1)} %or_bitcast_fusion), kind=kCustom, calls=%fused_computation | custom fusion | bytes 16778240 | tf_op jit(solution)/shard_map/gather | solution.py:180
  66.6 0.0 all-to-all-done.3
  66.6 0.0 copy-start.2
  66.6 0.0 copy-start
  66.6 0.0 copy-start.1
  66.7 9.7 %all-to-all-start.1 = ((bf16[128,1,128,256]{3,2,1,0:T(8,128)(2,1)}), bf16[128,1,128,256]{3,2,1,0:T(8,128)(2,1)}, u32[]{:S(2)}, u32[]{:S(2)}) async-start(bf16[128,1,128,256]{3,2,1,0:T(8,128)(2,1)} %bitcast.30), calls=%async_computation.1 | async-start | bytes 16777216 | tf_op jit(solution)/shard_map/all_to_all | solution.py:179
  76.3 0.0 copy-done.2
  76.3 0.1 copy.47
  76.5 0.6 reduce_sum.19
  77.1 0.2 reduce-window.8
  77.3 0.1 add_reduce_fusion
  77.4 0.1 select_reduce_fusion.index_ref
  77.5 1.1 copy.59
  78.6 117.2 %all-to-all-done.1 = bf16[128,1,128,256]{3,2,1,0:T(8,128)(2,1)} async-done(((bf16[128,1,128,256]{3,2,1,0:T(8,128)(2,1)}), bf16[128,1,128,256]{3,2,1,0:T(8,128)(2,1)}, u32[]{:S(2)}, u32[]{:S(2)}) %all-to-all-start.1) | async-done | bytes 8388640 | tf_op jit(solution)/shard_map/all_to_all | solution.py:179
  195.8 0.0 copy-done
  195.8 0.0 copy-done.1
  195.8 76.4 %shard_map.77 = bf16[768,1024]{1,0:T(8,128)(2,1)} custom-call(s32[32]{0:T(128)S(1)} %select_reduce_fusion.index_ref, s32[1]{0:T(128)} %bitcast.2.count_ref, bf16[768,1024]{1,0:T(8,128)(2,1)S(1)} %bitcast.29, bf16[768,256]{1,0:T(8,128)(2,1)S(1)} %bitcast.28, bf16[128,128,256]{2,1,0:T(8,128)(2,1)} %bitcast.11.pages_ref), custom_call_target="tpu_custom_call" | custom-call | flops 12884901888 | bytes 8388608 | tf_op jit(solution)/shard_map/pallas_call | solution.py:150
  (6 shorter events, 0.1 us)
Async XLA Ops:
  2.0 17.6 %all-to-all-start = ((s32[128,1,1]{2,1,0:T(1,128)}), s32[128,1,1]{2,1,0:T(1,128)S(1)}, u32[]{:S(2)}, u32[]{:S(2)}) async-start(s32[128,1,1]{2,1,0:T(1,128)} %copy.49), calls=%async_computation | async-start | bytes 131072 | tf_op jit(solution)/shard_map/all_to_all | solution.py:181
  38.8 27.8 %all-to-all-start.3 = ((bf16[16,128,256]{2,1,0:T(8,128)(2,1)}), bf16[16,128,256]{2,1,0:T(8,128)(2,1)S(1)}, u32[]{:S(2)}, u32[]{:S(2)}) async-start(bf16[16,128,256]{2,1,0:T(8,128)(2,1)} %all_to_all.37), calls=%async_computation.3 | async-start | bytes 2097152 | tf_op jit(solution)/shard_map/all_to_all | solution.py:197
  66.6 9.7 %copy-start.2 = (s32[1,128,1]{1,2,0:T(1,128)S(1)}, s32[1,128,1]{1,2,0:T(1,128)}, u32[]{:S(2)}) copy-start(s32[1,128,1]{1,2,0:T(1,128)} %param.10) | copy-start | bytes 1540
  66.6 129.2 %copy-start = (bf16[1,768,256]{2,1,0:T(8,128)(2,1)S(1)}, bf16[1,768,256]{2,1,0:T(8,128)(2,1)}, u32[]{:S(2)}) copy-start(bf16[1,768,256]{2,1,0:T(8,128)(2,1)} %param.7) | copy-start | bytes 1179652
  66.6 129.2 %copy-start.1 = (bf16[1,768,1024]{2,1,0:T(8,128)(2,1)S(1)}, bf16[1,768,1024]{2,1,0:T(8,128)(2,1)}, u32[]{:S(2)}) copy-start(bf16[1,768,1024]{2,1,0:T(8,128)(2,1)} %param.6) | copy-start | bytes 4718596
  66.7 129.1 %all-to-all-start.1 = ((bf16[128,1,128,256]{3,2,1,0:T(8,128)(2,1)}), bf16[128,1,128,256]{3,2,1,0:T(8,128)(2,1)}, u32[]{:S(2)}, u32[]{:S(2)}) async-start(bf16[128,1,128,256]{3,2,1,0:T(8,128)(2,1)} %bitcast.30), calls=%async_computation.1 | async-start | bytes 16777216 | tf_op jit(solution)/shard_map/all_to_all | solution.py:179

commit v2 on v1

v2 whole, which is shorter than its diff:
```python
import functools
import math

import jax
import jax.numpy as jnp
from jax import lax
from jax.experimental import pallas as pl
from jax.experimental.pallas import tpu as pltpu
from jax.sharding import PartitionSpec as P

HD = 128
PAGE = 128
CTXP = 32
QT = 256
KC = 512
LOG2E = 1.4426950408889634
NEG = -1e30


def compact_slots(live_flags):
    flat_live = live_flags.reshape(-1)
    live_rank = jnp.cumsum(flat_live) - 1
    slot_ids = jnp.arange(flat_live.shape[0], dtype=jnp.int32)
    targets = jnp.arange(CTXP, dtype=jnp.int32)
    select_table = (flat_live[None, :] == 1) & (live_rank[None, :] == targets[:, None])
    live_index = jnp.sum(jnp.where(select_table, slot_ids[None, :], 0), axis=1)
    return (live_index, jnp.sum(flat_live))


MESH = pl.DeviceIdType.MESH
CAP_Y, CAP_Z, CAP_X = 17, 27, 26
LISTS = 16


def coords():
    t, d = lax.axis_index("tp"), lax.axis_index("dec")
    return t, d, t % 4, (t // 4) * 2 + (d // 2) % 2, d // 4, d % 2


def flag(cond, dtype=jnp.float32):
    return jnp.where(cond, 1.0, 0.0).astype(dtype)


def table_kernel(row_ref, tab_ref, all_ref, send_sem, recv_sem):
    t, d, y, z, x, core = coords()
    n = 16
    barrier = pltpu.get_barrier_semaphore()
    for k in range(1, n):
        pl.semaphore_signal(barrier, inc=1, device_id={"dec": (d + k) % n}, device_id_type=MESH)
    pl.semaphore_wait(barrier, n - 1)

    def copy(k, slot):
        return pltpu.make_async_remote_copy(
            src_ref=row_ref,
            dst_ref=all_ref.at[slot],
            send_sem=send_sem.at[k],
            recv_sem=recv_sem.at[slot],
            device_id={"dec": (d + k) % n},
            device_id_type=MESH,
        )

    for k in range(1, n):
        copy(k, d).start()
    all_ref[d] = row_ref[...]

    bf16, f32 = jnp.bfloat16, jnp.float32
    oi = lax.broadcasted_iota(jnp.int32, (128, 128), 0)
    oj = lax.broadcasted_iota(jnp.int32, (128, 128), 1)
    gi = lax.broadcasted_iota(jnp.int32, (16, 16), 0)
    gj = lax.broadcasted_iota(jnp.int32, (16, 16), 1)
    group_z = lambda o: o & 0x4E
    group_x = lambda o: o & 0x0C
    owner_groups = (lambda o: o >> 1, group_z, group_x, lambda o: o & 0)
    asker_groups = (lambda g: g & 0, lambda g: g & 2, lambda g: g & 14, lambda g: g)

    for k in range(1, n):
        copy(k, (d + n - k) % n).wait_recv()
    packed = jnp.concatenate([all_ref[g, 0:1, :] for g in range(n)], axis=0)
    live = packed >= 0
    slot = jnp.maximum(packed, 0)
    flat = flag(live, bf16)

    ranks, counts = [], []
    for owner, asker in zip(owner_groups, asker_groups):
        same = owner(oi) == owner(oj)
        before = jnp.dot(flat, flag(same & (oi < oj), bf16), preferred_element_type=f32)
        total = jnp.dot(flat, flag(same, bf16), preferred_element_type=f32)
        side = asker(gi) == asker(gj)
        rank = jnp.dot(flag(side, bf16), before.astype(bf16), preferred_element_type=f32)
        rank += jnp.dot(flag(side & (gj < gi), bf16), flat, preferred_element_type=f32)
        ranks.append(rank.astype(jnp.int32))
        counts.append(jnp.dot(flag(side, bf16), total.astype(bf16), preferred_element_type=f32).astype(jnp.int32))

    o = lax.broadcasted_iota(jnp.int32, (16, 128), 1)
    g = lax.broadcasted_iota(jnp.int32, (16, 128), 0)
    o_x, o_y, o_z, o_c = (o >> 2) & 3, (o >> 4) & 3, ((o >> 6) << 1) | ((o >> 1) & 1), o & 1
    zlo = z % 2
    mine = (
        live & (o_x == x) & (o_y == y) & (o_z == z),
        live & (o_x == x) & (o_z == z),
        live & (o_x == x) & (((g >> 1) & 1) == zlo),
        live & ((g >> 1) == x * 2 + zlo),
    )
    values = (
        o_c * 8 + slot,
        o_y * CAP_Y + ranks[0],
        o_z * CAP_Z + ranks[1],
        o_x * CAP_X + ranks[2],
    )
    lists = (
        (range(16),),
        [[r for r in range(16) if (r >> 1) & 1 == b] for b in range(2)],
        [[r for r in range(16) if r >> 2 == b] for b in range(4)],
        [[r for r in range(16) if r & 1 == b] for b in range(2)],
    )
    place = lax.broadcasted_iota(jnp.int32, (CTXP, 128), 0)
    lane = lax.broadcasted_iota(jnp.int32, (CTXP, 128), 1)
    table = jnp.zeros((CTXP, 128), jnp.int32)
    column = 0
    for stage in range(4):
        rank = jnp.where(mine[stage], ranks[stage], -1)
        for rows in lists[stage]:
            found = jnp.zeros((CTXP, 128), jnp.int32)
            for r in rows:
                found += jnp.where(rank[r : r + 1, :] == place, values[stage][r : r + 1, :], 0)
            found = jnp.sum(found.astype(f32), axis=1, keepdims=True).astype(jnp.int32)
            table = jnp.where(lane == column, found, table)
            column += 1
    held = jnp.sum(flag(live & (g == d)).astype(f32)).astype(jnp.int32)
    over = jnp.maximum(
        jnp.maximum(jnp.max(counts[0]) - CAP_Y, jnp.max(counts[1]) - CAP_Z), jnp.max(counts[2]) - CAP_X
    )
    for c in range(2):
        size = jnp.sum(flag(live & (g == (d // 2) * 2 + c))).astype(jnp.int32)
        table = jnp.where((lane == 7 + c) & (place >= size), table[0:1, :], table)
    table = jnp.where(lane == 9, held, table)
    table = jnp.where(lane == 10, jnp.maximum(over, 0), table)
    square = jnp.concatenate([table.astype(f32), jnp.zeros((128 - CTXP, 128), f32)], axis=0)
    tab_ref[...] = jnp.transpose(square)[:LISTS, :].astype(jnp.int32)
    for k in range(1, n):
        copy(k, d).wait_send()


def make_table(cache_slot, cache_live):
    row = jnp.where(cache_live[0, :, 0] == 1, cache_slot[0, :, 0], -1)
    row = jnp.broadcast_to(row[None, :], (8, 128))
    vmem = pl.BlockSpec(memory_space=pltpu.VMEM)
    return pl.pallas_call(
        table_kernel,
        out_shape=jax.ShapeDtypeStruct((LISTS, 128), jnp.int32),
        in_specs=[vmem],
        out_specs=vmem,
        scratch_shapes=[
            pltpu.VMEM((16, 8, 128), jnp.int32),
            pltpu.SemaphoreType.DMA((16,)),
            pltpu.SemaphoreType.DMA((16,)),
        ],
        compiler_params=pltpu.CompilerParams(collective_id=0, has_side_effects=True),
    )(row)


NCH = 4
ROWS = 32


class Exchange:
    def __init__(self, tab, pool, span, pages, kv, refs, sems):
        self.tab, self.pool, self.span, self.pages, self.kv = tab, pool, span, pages, kv
        (self.pool16, self.send_y, self.recv_y, self.send_z, self.recv_z, self.send_x, self.recv_x, self.send_c,
         self.span_pad, self.send_d) = refs
        self.sems = sems
        self.t, self.d, self.y, self.z, self.x, self.core = coords()

    def barrier(self):
        t, d = self.t, self.d
        sem = pltpu.get_barrier_semaphore()
        for device in [self.peer("c", 1)] + [self.peer(a, k) for a in "yzx" for k in (1, 2, 3)]:
            pl.semaphore_signal(sem, inc=1, device_id=device, device_id_type=MESH)

        @pl.loop(0, 16)
        def _(n):
            ot, od = n // 2, t * 2 + n % 2

            @pl.when((ot != t) | (od != d))
            def _():
                pl.semaphore_signal(sem, inc=1, device_id={"tp": ot, "dec": od}, device_id_type=MESH)

        pl.semaphore_wait(sem, 26 - jnp.where(d // 2 == t, 1, 0))

    def peer(self, axis, k):
        t, d, y, z, x, c = self.t, self.d, self.y, self.z, self.x, self.core
        if axis == "c":
            c = 1 - c
        elif axis == "y":
            y = (y + k) % 4
        elif axis == "z":
            z = (z + k) % 4
        else:
            x = (x + k) % 4
        return {"tp": (z // 2) * 4 + y, "dec": x * 4 + (z % 2) * 2 + c}

    def remote(self, src, dst, send_sem, recv_sem, device):
        return pltpu.make_async_remote_copy(
            src_ref=src, dst_ref=dst, send_sem=send_sem, recv_sem=recv_sem, device_id=device, device_id_type=MESH
        )

    def pool_own(self, half):
        rows = pl.ds(self.core * 64 + half * ROWS, ROWS)
        return pltpu.make_async_copy(
            self.pool.at[:, rows, :], self.pool16[half].at[pl.ds(self.core * 8, 8)], self.sems["own"].at[half]
        )

    def pool_pair(self, half, into):
        rows = pl.ds((1 - self.core) * 64 + half * ROWS, ROWS)
        return self.remote(
            self.pool.at[:, rows, :],
            self.pool16[half].at[pl.ds(into * 8, 8)],
            self.sems["pair_send"].at[half],
            self.sems["pair_recv"].at[half],
            self.peer("c", 1),
        )

    def start_pool(self):
        for half in range(2):
            self.pool_own(half).start()
            self.pool_pair(half, self.core).start()

    def wait_pool(self, half):
        self.pool_own(half).wait()
        self.pool_pair(half, 1 - self.core).wait_recv()

    def hop(self, axis, ch, k, source):
        send, recv, stage = {
            "y": (self.send_y, self.recv_y, 0), "z": (self.send_z, self.recv_z, 1), "x": (self.send_x, self.recv_x, 2),
        }[axis]
        units = send.shape[2]
        return self.remote(
            send.at[ch, k - 1],
            recv[ch].at[pl.ds(source * units, units)],
            self.sems["send"].at[stage, ch, k - 1],
            self.sems["recv"].at[stage, ch, k - 1],
            self.peer(axis, k),
        )

    def start_hop(self, axis, ch):
        for k in (1, 2, 3):
            self.hop(axis, ch, k, getattr(self, axis)).start()

    def wait_hop(self, axis, ch):
        me = getattr(self, axis)
        for k in (1, 2, 3):
            self.hop(axis, ch, k, (me + 4 - k) % 4).wait_recv()

    def pack_y(self, ch):
        kv, half = ch // 2, ch % 2

        @pl.loop(0, CAP_Y)
        def _(n):
            slot = self.tab[0, n]
            for k in range(4):
                to = (self.y + k) % 4
                for zhi in range(2):
                    col = pl.multiple_of((zhi * 4 + to) * 256 + kv * HD, HD)
                    block = self.pool16[half][slot, :, pl.ds(col, HD)]
                    if k == 0:
                        self.recv_y[ch][self.y * (2 * CAP_Y) + n * 2 + zhi] = block
                    else:
                        self.send_y[ch, k - 1, n * 2 + zhi] = block

        self.start_hop("y", ch)

    def pack_z(self, ch):
        self.wait_hop("y", ch)

        @pl.loop(0, CAP_Z)
        def _(n):
            for k in range(4):
                to = (self.z + k) % 4
                block = self.recv_y[ch][self.tab[1 + to % 2, n] * 2 + to // 2]
                if k == 0:
                    self.recv_z[ch][self.z * CAP_Z + n] = block
                else:
                    self.send_z[ch, k - 1, n] = block

        self.start_hop("z", ch)

    def pack_x(self, ch):
        self.wait_hop("z", ch)

        @pl.loop(0, CAP_X)
        def _(n):
            for k in range(4):
                to = (self.x + k) % 4
                block = self.recv_z[ch][self.tab[3 + to, n]]
                if k == 0:
                    self.recv_x[ch][self.x * CAP_X + n] = block
                else:
                    self.send_x[ch, k - 1, n] = block

        self.start_hop("x", ch)

    def last(self, ch, lane):
        return self.remote(
            self.send_c.at[ch],
            self.kv[ch].at[lane],
            self.sems["last_send"].at[ch],
            self.sems["last_recv"].at[ch],
            self.peer("c", 1),
        )

    def pack_c(self, ch):
        self.wait_hop("x", ch)

        @pl.loop(0, CTXP)
        def _(n):
            rows = pl.ds(pl.multiple_of(n * ROWS, ROWS), ROWS)
            self.kv[ch][self.core, rows, :] = self.recv_x[ch][self.tab[7 + self.core, n]]
            self.send_c[ch, rows, :] = self.recv_x[ch][self.tab[8 - self.core, n]]

        self.last(ch, self.core).start()

    def wait_last(self, ch):
        self.last(ch, 1 - self.core).wait_recv()

    def new_page(self, n, ot, od, half, t):
        cols = pl.ds(pl.multiple_of(t * 256, 256), 256)
        return self.remote(
            self.send_d.at[n],
            self.pages.at[half, :, cols],
            self.sems["new_send"].at[n],
            self.sems["new_recv"].at[half * 8 + t],
            {"tp": ot, "dec": od},
        )

    def own_page(self):
        cols = pl.ds(pl.multiple_of(self.t * 256, 256), 256)
        return pltpu.make_async_copy(
            self.send_d.at[self.d], self.pages.at[self.d % 2, :, cols], self.sems["new_send"].at[self.d]
        )

    def start_new(self, dest):
        self.span_pad[0:6] = self.span[...].reshape(6, PAGE, 256)
        self.span_pad[6] = jnp.zeros((PAGE, 256), jnp.bfloat16)
        ot = self.d // 2

        @pl.loop(0, 16)
        def _(n):
            od = (self.d + n) % 16
            page = jnp.int32(6)
            for p in range(6):
                page = jnp.where(dest[p] == od, p, page)
            self.send_d[od] = self.span_pad[page]
            own = (ot == self.t) & (od == self.d)

            @pl.when(own)
            def _():
                self.own_page().start()

            @pl.when(jnp.logical_not(own))
            def _():
                self.new_page(od, ot, od, self.d % 2, self.t).start()

    def wait_new(self):
        t, d = self.t, self.d

        @pl.loop(0, 16)
        def _(n):
            st, half = n // 2, n % 2
            sd = t * 2 + half
            own = (st == t) & (sd == d)

            @pl.when(own)
            def _():
                self.own_page().wait()

            @pl.when(jnp.logical_not(own))
            def _():
                self.new_page(d, st, sd, half, st).wait_recv()

        @pl.loop(0, 16)
        def _(n):
            @pl.when((d // 2 != t) | (n != d))
            def _():
                self.new_page(n, d // 2, n, d % 2, t).wait_send()

    def wait_sends(self):
        for half in range(2):
            self.pool_pair(half, self.core).wait_send()
        for ch in range(NCH):
            for axis in "yzx":
                for k in (1, 2, 3):
                    self.hop(axis, ch, k, getattr(self, axis)).wait_send()
            self.last(ch, self.core).wait_send()


def exchange_scratch():
    bf16, vmem, dma = jnp.bfloat16, pltpu.VMEM, pltpu.SemaphoreType.DMA
    unit = (ROWS, HD)
    refs = [
        [vmem((16, ROWS, 2048), bf16) for _ in range(2)],
        vmem((NCH, 3, 2 * CAP_Y) + unit, bf16),
        [vmem((8 * CAP_Y,) + unit, bf16) for _ in range(NCH)],
        vmem((NCH, 3, CAP_Z) + unit, bf16),
        [vmem((4 * CAP_Z,) + unit, bf16) for _ in range(NCH)],
        vmem((NCH, 3, CAP_X) + unit, bf16),
        [vmem((4 * CAP_X,) + unit, bf16) for _ in range(NCH)],
        vmem((NCH, CTXP * ROWS, HD), bf16),
        vmem((7, PAGE, 256), bf16),
        vmem((16, PAGE, 256), bf16),
    ]
    sems = {
        "own": dma((2,)), "pair_send": dma((2,)), "pair_recv": dma((2,)), "send": dma((3, NCH, 3)),
        "recv": dma((3, NCH, 3)), "last_send": dma((NCH,)), "last_recv": dma((NCH,)), "new_send": dma((16,)),
        "new_recv": dma((16,)),
    }
    return refs, sems


def exchange_kernel(tab, dest, span, pool, k_out, v_out, pages, kv, refs, sems):
    ex = Exchange(tab, pool, span, pages, kv, refs, sems)
    ex.barrier()
    ex.start_pool()
    ex.start_new(dest)
    ex.wait_pool(0)
    ex.pack_y(0)
    ex.wait_pool(1)
    ex.pack_y(1)
    ex.pack_z(0)
    ex.pack_y(2)
    ex.pack_x(0)
    ex.pack_z(1)
    ex.pack_y(3)
    ex.pack_c(0)
    ex.pack_x(1)
    ex.pack_z(2)
    ex.pack_c(1)
    ex.pack_x(2)
    ex.pack_z(3)
    ex.pack_c(2)
    ex.pack_x(3)
    ex.pack_c(3)
    for ch in range(NCH):
        ex.wait_last(ch)
        out = (k_out, v_out)[ch // 2]
        out[pl.ds((ch % 2) * 2048, 2048), :] = kv[ch][...].reshape(2048, HD)
    ex.wait_new()
    ex.wait_sends()


def exchange(table, dest, span, pool):
    refs, sems = exchange_scratch()
    vmem = pl.BlockSpec(memory_space=pltpu.VMEM)
    smem = pl.BlockSpec(memory_space=pltpu.SMEM)
    hbm = pl.BlockSpec(memory_space=pl.ANY)
    bf16 = jnp.bfloat16
    keys = CTXP * PAGE
    return pl.pallas_call(
        exchange_kernel,
        out_shape=[
            jax.ShapeDtypeStruct((keys, HD), bf16),
            jax.ShapeDtypeStruct((keys, HD), bf16),
            jax.ShapeDtypeStruct((2, PAGE, 2048), bf16),
        ],
        in_specs=[smem, smem, vmem, hbm],
        out_specs=[vmem, vmem, hbm],
        scratch_shapes=[[pltpu.VMEM((2, CTXP * ROWS, HD), bf16) for _ in range(NCH)], refs, sems],
        compiler_params=pltpu.CompilerParams(
            collective_id=1, has_side_effects=True, vmem_limit_bytes=56 * 1024 * 1024
        ),
    )(table, dest, span, pool)


def attend_kernel(heads, span, tab_ref, q_ref, span_ref, k_in, v_in, out_ref, k_ref, v_ref, s_ref, mx_ref, acc_ref):
    cached = CTXP * PAGE
    tiles = span // QT
    coef = LOG2E / math.sqrt(HD)

    live = tab_ref[9, 0]
    k_ref[:cached, :] = k_in[...]
    k_ref[cached:, :] = span_ref[:, :HD]
    used = lax.broadcasted_iota(jnp.int32, (CTXP * 32, HD), 0) < live * 32
    for b in range(4):
        rows = pl.ds(b * CTXP * 32, CTXP * 32)
        v_ref[rows, :HD] = jnp.where(used, v_in[rows, :], 0).astype(jnp.bfloat16)
        v_ref[rows, HD:] = jnp.where(used, 1.0, 0.0).astype(jnp.bfloat16)
    v_ref[cached:, :HD] = span_ref[:, HD:]
    v_ref[cached:, HD:] = jnp.ones((span, HD), jnp.bfloat16)

    def q_tile(h, i):
        return q_ref[pl.ds(i * QT, QT), pl.ds(pl.multiple_of(h * HD, HD), HD)]

    def fold(part, width):
        out = part[:, :HD]
        for c in range(1, width // HD):
            out = jnp.maximum(out, part[:, c * HD : (c + 1) * HD])
        return out

    def score(slot, q, start, width, mask=None):
        part = lax.dot_general(
            q, k_ref[pl.ds(start, width), :], (((1,), (1,)), ((), ())), preferred_element_type=jnp.float32
        )
        if mask is not None:
            part = jnp.where(mask, part, NEG)
        s_ref[slot, :, pl.ds(start, width)] = part
        mx_ref[slot] = jnp.maximum(mx_ref[slot], fold(part, width))

    def mix(slot, top, start, width):
        part = s_ref[slot, :, pl.ds(start, width)]
        weights = [
            jnp.exp2((part[:, c * HD : (c + 1) * HD] - top) * coef).astype(jnp.bfloat16) for c in range(width // HD)
        ]
        acc_ref[...] += jnp.dot(
            jnp.concatenate(weights, axis=1), v_ref[pl.ds(start, width), :], preferred_element_type=jnp.float32
        )

    def diagonal_mask():
        return lax.broadcasted_iota(jnp.int32, (QT, QT), 1) <= lax.broadcasted_iota(jnp.int32, (QT, QT), 0)

    def step(score_of, mix_of):
        if score_of is not None:
            sh, si, ss = score_of
            q = q_tile(sh, si)
            mx_ref[ss] = jnp.full((QT, HD), NEG, jnp.float32)
        if mix_of is not None:
            mh, mi, ms = mix_of
            top = jnp.broadcast_to(jnp.max(mx_ref[ms], axis=1, keepdims=True), (QT, HD))
            acc_ref[...] = jnp.zeros_like(acc_ref)

        @pl.loop(0, cached // KC)
        def _(j):
            start = pl.multiple_of(j * KC, KC)
            if score_of is not None:
                score(ss, q, start, KC)
            if mix_of is not None:
                mix(ms, top, start, KC)

        if score_of is not None:
            for b in range(si):
                score(ss, q, cached + b * QT, QT)
            score(ss, q, cached + si * QT, QT, diagonal_mask())
        if mix_of is not None:
            mix(ms, top, cached, (mi + 1) * QT)
            acc = acc_ref[...]
            out_ref[pl.ds(mi * QT, QT), pl.ds(pl.multiple_of(mh * HD, HD), HD)] = (
                acc[:, :HD] / acc[:, HD:]
            ).astype(out_ref.dtype)

    step((0, 0, 0), None)

    @pl.loop(0, heads // 2)
    def _(hh):
        for n in range(2 * tiles):
            now = (hh * 2 + n // tiles, n % tiles, n % 2)
            m = n + 1
            later = (jnp.minimum(hh * 2 + m // tiles, heads - 1), m % tiles, m % 2)
            step(later, now)


def attend(queries, span_kv, table, keys, values):
    span, width = queries.shape
    heads = width // HD
    cached = CTXP * PAGE
    vmem = pl.BlockSpec(memory_space=pltpu.VMEM)
    smem = pl.BlockSpec(memory_space=pltpu.SMEM)
    return pl.pallas_call(
        functools.partial(attend_kernel, heads, span),
        out_shape=jax.ShapeDtypeStruct((span, width), jnp.bfloat16),
        in_specs=[smem, vmem, vmem, vmem, vmem],
        out_specs=vmem,
        scratch_shapes=[
            pltpu.VMEM((cached + span, HD), jnp.bfloat16),
            pltpu.VMEM((cached + span, 2 * HD), jnp.bfloat16),
            pltpu.VMEM((2, QT, cached + span), jnp.float32),
            pltpu.VMEM((2, QT, HD), jnp.float32),
            pltpu.VMEM((QT, 2 * HD), jnp.float32),
        ],
        compiler_params=pltpu.CompilerParams(vmem_limit_bytes=48 * 1024 * 1024),
        cost_estimate=pl.CostEstimate(
            flops=4 * span * width * cached, bytes_accessed=8 * 1024 * 1024, transcendentals=span * heads * cached
        ),
    )(table, queries, span_kv, keys, values)


def dense_exchange(table, dest, span, pool, slots, flags):
    tp_size, dec_size = lax.axis_size("tp"), lax.axis_size("dec")
    devices = tp_size * dec_size
    width = span.shape[1]
    view = pool.reshape(pool.shape[0], PAGE, tp_size, width)
    source_rows = (jnp.arange(devices, dtype=jnp.int32) // dec_size)[:, None]
    axes = ("tp", "dec")
    asked = lax.all_to_all(slots, axes, split_axis=0, concat_axis=0, tiled=True)
    fetched = lax.all_to_all(view[asked, :, source_rows], axes, split_axis=0, concat_axis=0, tiled=True)
    live_index, live_count = compact_slots(flags)
    live_index = jnp.where(jnp.arange(CTXP) < live_count, live_index, live_index[0])
    cached = fetched.reshape(devices, PAGE, width)[live_index].reshape(CTXP, 2, 2, 32, 2, HD)
    cached = jnp.transpose(cached, (4, 2, 1, 0, 3, 5)).reshape(2, CTXP * PAGE, HD)
    new_pages = span.reshape(-1, PAGE, width)
    chosen = (dest[None, :] == jnp.arange(dec_size, dtype=jnp.int32)[:, None]).astype(jnp.bfloat16)
    outgoing = jnp.einsum("dp,pkc->dkc", chosen, new_pages, preferred_element_type=jnp.float32).astype(jnp.bfloat16)
    placed = lax.all_to_all(outgoing, "dec", split_axis=0, concat_axis=0, tiled=True)
    placed = lax.all_to_all(placed, "tp", split_axis=0, concat_axis=2, tiled=True)
    return (cached[0], cached[1], placed)


def body(queries, span_kv, page_pool, cache_slot, cache_live, span_dest):
    table = make_table(cache_slot, cache_live)
    keys, values, placed = lax.cond(
        table[10, 0] > 0,
        lambda tab, dest, span, pool, slots, flags: dense_exchange(tab, dest, span, pool, slots, flags),
        lambda tab, dest, span, pool, slots, flags: tuple(exchange(tab, dest, span, pool)),
        table, span_dest[0], span_kv[0], page_pool, cache_slot[0], cache_live[0],
    )
    attn_out = attend(queries[0], span_kv[0], table, keys, values)[None]
    return (attn_out, placed)


def solution(mesh):
    in_specs = (
        P("dec", None, "tp"),
        P("dec", None, "tp"),
        P(("tp", "dec"), None, None),
        P("dec", None, None),
        P("dec", None, None),
        P("dec", None),
    )
    out_specs = (P("dec", None, "tp"), P(("tp", "dec"), None, None))
    return jax.shard_map(body, mesh=mesh, in_specs=in_specs, out_specs=out_specs, check_vma=False)
```

time: 273 us -> 207 us (0.76)
  the two profiles are of different devices: /device:TPU:12 before, /device:TPU:1 now
where the time goes in v2:
time: 207 us
  Pallas kernels  203 us (98%)
  local copies, waits for them, and re-layouts  2.08 us (1%)
    pallas_call x1, Pallas kernels, exchange(): pl.pallas_call(exchange_kernel, out_shape=[jax.ShapeDtypeStruct((keys, HD...  117 us
    pallas_call x1, Pallas kernels, attend(): pl.pallas_call(functools.partial(attend_kernel, heads, span), out_shape=j...  75.2 us
    pallas_call x1, Pallas kernels, make_table(): pl.pallas_call(table_kernel, out_shape=jax.ShapeDtypeStruct((LISTS, 128),...  10.3 us

profile of v2, /device:TPU:1, one launch (start us, length us, event | category | flops | bytes accessed | tf_op | source)
XLA Modules:
  0.0 207.1 jit_solution(12316054935594201340)
XLA Ops:
  0.6 0.7 fusion.6
  1.3 0.6 broadcast_in_dim.38.row_ref
  1.9 10.3 %shard_map.77.tab_ref = s32[16,128]{1,0:T(8,128)S(1)} custom-call(s32[8,128]{1,0:T(8,128)} %broadcast_in_dim.38.row_ref), custom_call_target="tpu_custom_call" | custom-call | tf_op jit(solution)/shard_map/pallas_call | solution.py:148
  12.2 0.5 slice.14
  13.4 0.0 copy-start
  13.4 117.4 %conditional.1 = ((bf16[4096,128]{1,0:T(8,128)(2,1)}, bf16[4096,128]{1,0:T(8,128)(2,1)}, bf16[2,128,2048]{2,1,0:T(8,128)(2,1)S(1)})) conditional(s32[]{:T(128)} %bitcast.24, (s32[1,6]{1,0:T(1,128)}, s32[16,128]{1,0:T(8,128)S(1)}, bf16[768,256]{1,0:T(8,128)(2,1)}, bf16[8,128,2048]{2,1,0:T(8,128)(2,1)}) %tuple.30, (bf16[8,128,2048]{2,1,0:T(8,128)(2,1)}, ...), branch_computations={%region_0.1_spmd, %region_1.5_spmd} | conditional | flops 6854751 | bytes 90727016 | solution.py:607
  13.4 117.2 %branch_0_fun.1 = (bf16[4096,128]{1,0:T(8,128)(2,1)}, bf16[4096,128]{1,0:T(8,128)(2,1)}, bf16[2,128,2048]{2,1,0:T(8,128)(2,1)S(1)}) custom-call(s32[16,128]{1,0:T(8,128)S(1)} %get-tuple-element.19.tab, s32[6]{0:T(128)} %bitcast.50, bf16[768,256]{1,0:T(8,128)(2,1)} %get-tuple-element.21.span, bf16[8,128,2048]{2,1,0:T(8,128)(2,1)} %get-tuple-element.22.pool), custom_call_target="tpu_custom_call" | custom-call | tf_op jit(solution)/shard_map/cond/branch_0_fun/pallas_call | solution.py:457
  130.8 0.0 copy-done
  130.8 75.2 %shard_map.78 = bf16[768,1024]{1,0:T(8,128)(2,1)} custom-call(s32[16,128]{1,0:T(8,128)S(1)} %shard_map.77.tab_ref, bf16[768,1024]{1,0:T(8,128)(2,1)S(1)} %bitcast.41, bf16[768,256]{1,0:T(8,128)(2,1)} %bitcast.47, bf16[4096,128]{1,0:T(8,128)(2,1)} %get-tuple-element.33.k_in, bf16[4096,128]{1,0:T(8,128)(2,1)} %get-tuple-element.34.v_in), custom_call_target="tpu_custom_call" | custom-call | flops 12884901888 | bytes 8388608 | tf_op jit(solution)/shard_map/pallas_call | solution.py:565
  206.1 1.0 copy.79
Async XLA Ops:
  13.4 117.5 %copy-start = (bf16[1,768,1024]{2,1,0:T(8,128)(2,1)S(1)}, bf16[1,768,1024]{2,1,0:T(8,128)(2,1)}, u32[]{:S(2)}) copy-start(bf16[1,768,1024]{2,1,0:T(8,128)(2,1)} %param.8) | copy-start | bytes 4718596

commit v3 on v2

--- a/solution.py
+++ b/solution.py
@@ -11,8 +11,6 @@
 HD = 128
 PAGE = 128
 CTXP = 32
-QT = 256
-KC = 512
 LOG2E = 1.4426950408889634
 NEG = -1e30
 
@@ -28,7 +26,7 @@
 
 
 MESH = pl.DeviceIdType.MESH
-CAP_Y, CAP_Z, CAP_X = 17, 27, 26
+CAP_Y, CAP_Z, CAP_X = 13, 25, 26
 LISTS = 16
 
 
@@ -68,48 +66,61 @@
     oj = lax.broadcasted_iota(jnp.int32, (128, 128), 1)
     gi = lax.broadcasted_iota(jnp.int32, (16, 16), 0)
     gj = lax.broadcasted_iota(jnp.int32, (16, 16), 1)
-    group_z = lambda o: o & 0x4E
-    group_x = lambda o: o & 0x0C
-    owner_groups = (lambda o: o >> 1, group_z, group_x, lambda o: o & 0)
-    asker_groups = (lambda g: g & 0, lambda g: g & 2, lambda g: g & 14, lambda g: g)
+    owner_groups = (lambda o: o >> 1, lambda o: o & 0x4E, lambda o: o & 0x0C, lambda o: o & 0)
+    row_groups = (lambda g: g & 0, lambda g: g >> 3, lambda g: g & 14, lambda g: g)
 
     for k in range(1, n):
         copy(k, (d + n - k) % n).wait_recv()
     packed = jnp.concatenate([all_ref[g, 0:1, :] for g in range(n)], axis=0)
-    live = packed >= 0
-    slot = jnp.maximum(packed, 0)
-    flat = flag(live, bf16)
+    o = lax.broadcasted_iota(jnp.int32, (16, 128), 1)
+    g = lax.broadcasted_iota(jnp.int32, (16, 128), 0)
+    g_zlo = (g >> 1) & 1
+    asked = [
+        [jnp.max(flag((packed == s) & (g_zlo == b)), axis=0, keepdims=True) for s in range(8)] for b in range(2)
+    ]
+    by_slot = [jnp.maximum(p, q) for p, q in zip(*asked)]
+    wants = (
+        jnp.concatenate(by_slot + [jnp.zeros((8, 128), f32)], axis=0).astype(bf16),
+        jnp.concatenate(asked[0] + asked[1], axis=0).astype(bf16),
+        flag(packed >= 0, bf16),
+        flag(packed >= 0, bf16),
+    )
 
     ranks, counts = [], []
-    for owner, asker in zip(owner_groups, asker_groups):
+    for want, owner, row in zip(wants, owner_groups, row_groups):
         same = owner(oi) == owner(oj)
-        before = jnp.dot(flat, flag(same & (oi < oj), bf16), preferred_element_type=f32)
-        total = jnp.dot(flat, flag(same, bf16), preferred_element_type=f32)
-        side = asker(gi) == asker(gj)
+        before = jnp.dot(want, flag(same & (oi < oj), bf16), preferred_element_type=f32)
+        total = jnp.dot(want, flag(same, bf16), preferred_element_type=f32)
+        side = row(gi) == row(gj)
         rank = jnp.dot(flag(side, bf16), before.astype(bf16), preferred_element_type=f32)
-        rank += jnp.dot(flag(side & (gj < gi), bf16), flat, preferred_element_type=f32)
+        rank += jnp.dot(flag(side & (gj < gi), bf16), want, preferred_element_type=f32)
         ranks.append(rank.astype(jnp.int32))
         counts.append(jnp.dot(flag(side, bf16), total.astype(bf16), preferred_element_type=f32).astype(jnp.int32))
 
-    o = lax.broadcasted_iota(jnp.int32, (16, 128), 1)
-    g = lax.broadcasted_iota(jnp.int32, (16, 128), 0)
+    rank_y = jnp.concatenate([ranks[0][0:8], ranks[0][0:8]], axis=0)
+    rank_z = jnp.zeros((16, 128), jnp.int32)
+    for s in range(8):
+        row = jnp.where(g_zlo == 1, ranks[1][8 + s : 9 + s, :], ranks[1][s : s + 1, :])
+        rank_z = jnp.where(packed == s, row, rank_z)
+
     o_x, o_y, o_z, o_c = (o >> 2) & 3, (o >> 4) & 3, ((o >> 6) << 1) | ((o >> 1) & 1), o & 1
     zlo = z % 2
-    mine = (
-        live & (o_x == x) & (o_y == y) & (o_z == z),
-        live & (o_x == x) & (o_z == z),
-        live & (o_x == x) & (((g >> 1) & 1) == zlo),
-        live & ((g >> 1) == x * 2 + zlo),
+    places = (
+        (o_x == x) & (o_y == y) & (o_z == z),
+        (o_x == x) & (o_z == z),
+        (o_x == x) & (g_zlo == zlo),
+        (g >> 1) == x * 2 + zlo,
     )
+    mine = [(want.astype(f32) > 0) & place for want, place in zip(wants, places)]
     values = (
-        o_c * 8 + slot,
-        o_y * CAP_Y + ranks[0],
-        o_z * CAP_Z + ranks[1],
+        o_c * 8 + g,
+        o_y * CAP_Y + rank_y,
+        o_z * CAP_Z + rank_z,
         o_x * CAP_X + ranks[2],
     )
     lists = (
-        (range(16),),
-        [[r for r in range(16) if (r >> 1) & 1 == b] for b in range(2)],
+        (range(8),),
+        (range(8), range(8, 16)),
         [[r for r in range(16) if r >> 2 == b] for b in range(4)],
         [[r for r in range(16) if r & 1 == b] for b in range(2)],
     )
@@ -126,7 +137,8 @@
             found = jnp.sum(found.astype(f32), axis=1, keepdims=True).astype(jnp.int32)
             table = jnp.where(lane == column, found, table)
             column += 1
-    held = jnp.sum(flag(live & (g == d)).astype(f32)).astype(jnp.int32)
+    live = packed >= 0
+    held = jnp.sum(flag(live & (g == d))).astype(jnp.int32)
     over = jnp.maximum(
         jnp.maximum(jnp.max(counts[0]) - CAP_Y, jnp.max(counts[1]) - CAP_Z), jnp.max(counts[2]) - CAP_X
     )
@@ -159,8 +171,10 @@
     )(row)
 
 
-NCH = 4
-ROWS = 32
+QUARTERS = 4
+NCH = 2 * QUARTERS
+ROWS = 16
+BLOCK = 2 * CTXP * ROWS
 
 
 class Exchange:
@@ -221,7 +235,7 @@
         )
 
     def start_pool(self):
-        for half in range(2):
+        for half in range(QUARTERS):
             self.pool_own(half).start()
             self.pool_pair(half, self.core).start()
 
@@ -252,7 +266,7 @@
             self.hop(axis, ch, k, (me + 4 - k) % 4).wait_recv()
 
     def pack_y(self, ch):
-        kv, half = ch // 2, ch % 2
+        half, kv = ch // 2, ch % 2
 
         @pl.loop(0, CAP_Y)
         def _(n):
@@ -302,7 +316,7 @@
     def last(self, ch, lane):
         return self.remote(
             self.send_c.at[ch],
-            self.kv[ch].at[lane],
+            self.kv.at[ch, pl.ds(lane * CTXP * ROWS, CTXP * ROWS)],
             self.sems["last_send"].at[ch],
             self.sems["last_recv"].at[ch],
             self.peer("c", 1),
@@ -314,7 +328,8 @@
         @pl.loop(0, CTXP)
         def _(n):
             rows = pl.ds(pl.multiple_of(n * ROWS, ROWS), ROWS)
-            self.kv[ch][self.core, rows, :] = self.recv_x[ch][self.tab[7 + self.core, n]]
+            own = pl.ds(pl.multiple_of((self.core * CTXP + n) * ROWS, ROWS), ROWS)
+            self.kv[ch, own, :] = self.recv_x[ch][self.tab[7 + self.core, n]]
             self.send_c[ch, rows, :] = self.recv_x[ch][self.tab[8 - self.core, n]]
 
         self.last(ch, self.core).start()
@@ -384,7 +399,7 @@
                 self.new_page(n, d // 2, n, d % 2, t).wait_send()
 
     def wait_sends(self):
-        for half in range(2):
+        for half in range(QUARTERS):
             self.pool_pair(half, self.core).wait_send()
         for ch in range(NCH):
             for axis in "yzx":
@@ -397,7 +412,7 @@
     bf16, vmem, dma = jnp.bfloat16, pltpu.VMEM, pltpu.SemaphoreType.DMA
     unit = (ROWS, HD)
     refs = [
-        [vmem((16, ROWS, 2048), bf16) for _ in range(2)],
+        [vmem((16, ROWS, 2048), bf16) for _ in range(QUARTERS)],
         vmem((NCH, 3, 2 * CAP_Y) + unit, bf16),
         [vmem((8 * CAP_Y,) + unit, bf16) for _ in range(NCH)],
         vmem((NCH, 3, CAP_Z) + unit, bf16),
@@ -409,179 +424,225 @@
         vmem((16, PAGE, 256), bf16),
     ]
     sems = {
-        "own": dma((2,)), "pair_send": dma((2,)), "pair_recv": dma((2,)), "send": dma((3, NCH, 3)),
+        "own": dma((QUARTERS,)), "pair_send": dma((QUARTERS,)), "pair_recv": dma((QUARTERS,)), "send": dma((3, NCH, 3)),
         "recv": dma((3, NCH, 3)), "last_send": dma((NCH,)), "last_recv": dma((NCH,)), "new_send": dma((16,)),
         "new_recv": dma((16,)),
     }
     return refs, sems
 
 
-def exchange_kernel(tab, dest, span, pool, k_out, v_out, pages, kv, refs, sems):
+class Attention:
+    def __init__(self, q, out, s, mx, m, acc):
+        self.q, self.out, self.s, self.mx, self.m, self.acc = q, out, s, mx, m, acc
+        self.span = q.shape[0]
+        self.heads = q.shape[1] // HD
+        self.coef = LOG2E / math.sqrt(HD)
+
+    def columns(self, n):
+        return pl.ds(pl.multiple_of(n * HD, HD), HD)
+
+    def score(self, n, slot, k, mask=None):
+        q = self.q[:, self.columns(n)]
+        width = k.shape[0]
+        step = min(512, width)
+        top = None
+        for start in range(0, width, step):
+            size = min(step, width - start)
+            part = lax.dot_general(
+                q, k[start : start + size], (((1,), (1,)), ((), ())), preferred_element_type=jnp.float32
+            )
+            if mask is not None:
+                part = jnp.where(mask[:, start : start + size], part, NEG)
+            self.s[slot][:, start : start + size] = part
+            for c in range(0, size, HD):
+                piece = part[:, c : c + HD]
+                top = piece if top is None else jnp.maximum(top, piece)
+        self.mx[slot][...] = top
+
+    def mix(self, n, slot, v, first):
+        top = jnp.broadcast_to(jnp.max(self.mx[slot][...], axis=1, keepdims=True), (self.span, HD))
+        if not first:
+            old = self.m[n]
+            top = jnp.maximum(old, top)
+            fade = jnp.exp2((old - top) * self.coef)
+        self.m[n] = top
+        weights = [
+            jnp.exp2((self.s[slot][:, c : c + HD] - top) * self.coef).astype(jnp.bfloat16)
+            for c in range(0, v.shape[0], HD)
+        ]
+        mixed = jnp.dot(jnp.concatenate(weights, axis=1), v, preferred_element_type=jnp.float32)
+        if not first:
+            mixed += self.acc[n] * jnp.concatenate([fade, fade], axis=1)
+        self.acc[n] = mixed
+
+    def two_heads(self, pair, k, v, first=False, mask=None):
+        n = pair * 2
+        self.score(n + 1, 1, k, mask)
+        self.mix(n, 0, v, first)
+        self.score(jnp.minimum(n + 2, self.heads - 1), 0, k, mask)
+        self.mix(n + 1, 1, v, first)
+
+    def causal(self):
+        shape = (self.span, self.span)
+        return lax.broadcasted_iota(jnp.int32, shape, 1) <= lax.broadcasted_iota(jnp.int32, shape, 0)
+
+    def finish(self):
+        @pl.loop(0, self.heads)
+        def _(n):
+            acc = self.acc[n]
+            self.out[:, self.columns(n)] = (acc[:, :HD] / acc[:, HD:]).astype(self.out.dtype)
+
+
+def attention_scratch(span, width):
+    heads = width // HD
+    wide = max(BLOCK, span)
+    f32 = jnp.float32
+    return [
+        [pltpu.VMEM((span, wide), f32) for _ in range(2)],
+        [pltpu.VMEM((span, HD), f32) for _ in range(2)],
+        pltpu.VMEM((heads, span, HD), f32),
+        pltpu.VMEM((heads, span, 2 * HD), f32),
+    ]
+
+
+def value_block(values, live):
+    row = lax.broadcasted_iota(jnp.int32, (BLOCK, HD), 0) % (CTXP * ROWS)
+    used = row < live * ROWS
+    return jnp.where(used, values, 0).astype(jnp.bfloat16), jnp.where(used, 1.0, 0.0).astype(jnp.bfloat16)
+
+
+def span_values(span_ref, v_span):
+    v_span[:, :HD] = span_ref[:, HD:]
+    v_span[:, HD:] = jnp.ones((v_span.shape[0], HD), jnp.bfloat16)
+
+
+def fused_kernel(tab, dest, q, span, pool, out, pages, kv, v_span, v_block, attn, refs, sems):
     ex = Exchange(tab, pool, span, pages, kv, refs, sems)
+    at = Attention(q, out, *attn)
+    pairs = at.heads // 2
+    first_block = 8
+
     ex.barrier()
     ex.start_pool()
-    ex.start_new(dest)
-    ex.wait_pool(0)
-    ex.pack_y(0)
-    ex.wait_pool(1)
-    ex.pack_y(1)
-    ex.pack_z(0)
-    ex.pack_y(2)
-    ex.pack_x(0)
-    ex.pack_z(1)
-    ex.pack_y(3)
-    ex.pack_c(0)
-    ex.pack_x(1)
-    ex.pack_z(2)
-    ex.pack_c(1)
-    ex.pack_x(2)
-    ex.pack_z(3)
-    ex.pack_c(2)
-    ex.pack_x(3)
-    ex.pack_c(3)
-    for ch in range(NCH):
-        ex.wait_last(ch)
-        out = (k_out, v_out)[ch // 2]
-        out[pl.ds((ch % 2) * 2048, 2048), :] = kv[ch][...].reshape(2048, HD)
+    span_values(span, v_span)
+    at.score(0, 0, span[:, :HD], at.causal())
+
+    @pl.loop(0, first_block + QUARTERS * pairs)
+    def _(step):
+        for i in range(NCH + 3):
+
+            @pl.when(step == 2 * i)
+            def _(i=i):
+                if i == 0:
+                    ex.wait_pool(0)
+                    ex.pack_y(0)
+                if 0 <= i - 3 < NCH:
+                    ex.pack_c(i - 3)
+                if 0 <= i - 2 < NCH:
+                    ex.pack_x(i - 2)
+                if 0 <= i - 1 < NCH:
+                    ex.pack_z(i - 1)
+                if i + 1 < NCH:
+                    if i % 2 == 1:
+                        ex.wait_pool((i + 1) // 2)
+                    ex.pack_y(i + 1)
+                if i == NCH:
+                    ex.start_new(dest)
+
+        @pl.when(step < pairs)
+        def _():
+            at.two_heads(step, span[:, :HD], v_span[...], True, at.causal())
+
+        for b in range(QUARTERS):
+
+            @pl.when(step == first_block + b * pairs)
+            def _(b=b):
+                ex.wait_last(2 * b)
+                ex.wait_last(2 * b + 1)
+                values, ones = value_block(kv[2 * b + 1], tab[9, 0])
+                v_block[:, :HD] = values
+                v_block[:, HD:] = ones
+                at.score(0, 0, kv[2 * b])
+
+        @pl.when(step >= first_block)
+        def _():
+            e = step - first_block
+            at.two_heads(e % pairs, kv[(e // pairs) * 2], v_block[...])
+
+    at.finish()
     ex.wait_new()
     ex.wait_sends()
 
 
-def exchange(table, dest, span, pool):
+def fused(table, dest, queries, span, pool):
     refs, sems = exchange_scratch()
     vmem = pl.BlockSpec(memory_space=pltpu.VMEM)
     smem = pl.BlockSpec(memory_space=pltpu.SMEM)
     hbm = pl.BlockSpec(memory_space=pl.ANY)
     bf16 = jnp.bfloat16
-    keys = CTXP * PAGE
+    rows, width = queries.shape
     return pl.pallas_call(
-        exchange_kernel,
-        out_shape=[
-            jax.ShapeDtypeStruct((keys, HD), bf16),
-            jax.ShapeDtypeStruct((keys, HD), bf16),
-            jax.ShapeDtypeStruct((2, PAGE, 2048), bf16),
+        fused_kernel,
+        out_shape=[jax.ShapeDtypeStruct((rows, width), bf16), jax.ShapeDtypeStruct((2, PAGE, 2048), bf16)],
+        in_specs=[smem, smem, vmem, vmem, hbm],
+        out_specs=[vmem, hbm],
+        scratch_shapes=[
+            pltpu.VMEM((NCH, BLOCK, HD), bf16),
+            pltpu.VMEM((rows, 2 * HD), bf16),
+            pltpu.VMEM((BLOCK, 2 * HD), bf16),
+            attention_scratch(rows, width),
+            refs,
+            sems,
         ],
-        in_specs=[smem, smem, vmem, hbm],
-        out_specs=[vmem, vmem, hbm],
-        scratch_shapes=[[pltpu.VMEM((2, CTXP * ROWS, HD), bf16) for _ in range(NCH)], refs, sems],
         compiler_params=pltpu.CompilerParams(
-            collective_id=1, has_side_effects=True, vmem_limit_bytes=56 * 1024 * 1024
+            collective_id=1, has_side_effects=True, vmem_limit_bytes=62 * 1024 * 1024
         ),
-    )(table, dest, span, pool)
-
-
-def attend_kernel(heads, span, tab_ref, q_ref, span_ref, k_in, v_in, out_ref, k_ref, v_ref, s_ref, mx_ref, acc_ref):
-    cached = CTXP * PAGE
-    tiles = span // QT
-    coef = LOG2E / math.sqrt(HD)
-
-    live = tab_ref[9, 0]
-    k_ref[:cached, :] = k_in[...]
-    k_ref[cached:, :] = span_ref[:, :HD]
-    used = lax.broadcasted_iota(jnp.int32, (CTXP * 32, HD), 0) < live * 32
-    for b in range(4):
-        rows = pl.ds(b * CTXP * 32, CTXP * 32)
-        v_ref[rows, :HD] = jnp.where(used, v_in[rows, :], 0).astype(jnp.bfloat16)
-        v_ref[rows, HD:] = jnp.where(used, 1.0, 0.0).astype(jnp.bfloat16)
-    v_ref[cached:, :HD] = span_ref[:, HD:]
-    v_ref[cached:, HD:] = jnp.ones((span, HD), jnp.bfloat16)
-
-    def q_tile(h, i):
-        return q_ref[pl.ds(i * QT, QT), pl.ds(pl.multiple_of(h * HD, HD), HD)]
-
-    def fold(part, width):
-        out = part[:, :HD]
-        for c in range(1, width // HD):
-            out = jnp.maximum(out, part[:, c * HD : (c + 1) * HD])
-        return out
-
-    def score(slot, q, start, width, mask=None):
-        part = lax.dot_general(
-            q, k_ref[pl.ds(start, width), :], (((1,), (1,)), ((), ())), preferred_element_type=jnp.float32
-        )
-        if mask is not None:
-            part = jnp.where(mask, part, NEG)
-        s_ref[slot, :, pl.ds(start, width)] = part
-        mx_ref[slot] = jnp.maximum(mx_ref[slot], fold(part, width))
-
-    def mix(slot, top, start, width):
-        part = s_ref[slot, :, pl.ds(start, width)]
-        weights = [
-            jnp.exp2((part[:, c * HD : (c + 1) * HD] - top) * coef).astype(jnp.bfloat16) for c in range(width // HD)
-        ]
-        acc_ref[...] += jnp.dot(
-            jnp.concatenate(weights, axis=1), v_ref[pl.ds(start, width), :], preferred_element_type=jnp.float32
-        )
-
-    def diagonal_mask():
-        return lax.broadcasted_iota(jnp.int32, (QT, QT), 1) <= lax.broadcasted_iota(jnp.int32, (QT, QT), 0)
-
-    def step(score_of, mix_of):
-        if score_of is not None:
-            sh, si, ss = score_of
-            q = q_tile(sh, si)
-            mx_ref[ss] = jnp.full((QT, HD), NEG, jnp.float32)
-        if mix_of is not None:
-            mh, mi, ms = mix_of
-            top = jnp.broadcast_to(jnp.max(mx_ref[ms], axis=1, keepdims=True), (QT, HD))
-            acc_ref[...] = jnp.zeros_like(acc_ref)
-
-        @pl.loop(0, cached // KC)
-        def _(j):
-            start = pl.multiple_of(j * KC, KC)
-            if score_of is not None:
-                score(ss, q, start, KC)
-            if mix_of is not None:
-                mix(ms, top, start, KC)
-
-        if score_of is not None:
-            for b in range(si):
-                score(ss, q, cached + b * QT, QT)
-            score(ss, q, cached + si * QT, QT, diagonal_mask())
-        if mix_of is not None:
-            mix(ms, top, cached, (mi + 1) * QT)
-            acc = acc_ref[...]
-            out_ref[pl.ds(mi * QT, QT), pl.ds(pl.multiple_of(mh * HD, HD), HD)] = (
-                acc[:, :HD] / acc[:, HD:]
-            ).astype(out_ref.dtype)
-
-    step((0, 0, 0), None)
-
-    @pl.loop(0, heads // 2)
-    def _(hh):
-        for n in range(2 * tiles):
-            now = (hh * 2 + n // tiles, n % tiles, n % 2)
-            m = n + 1
-            later = (jnp.minimum(hh * 2 + m // tiles, heads - 1), m % tiles, m % 2)
-            step(later, now)
-
-
-def attend(queries, span_kv, table, keys, values):
-    span, width = queries.shape
-    heads = width // HD
-    cached = CTXP * PAGE
+    )(table, dest, queries, span, pool)
+
+
+def attend_kernel(tab, q, span, kv, out, v_span, v_block, attn):
+    at = Attention(q, out, *attn)
+    pairs = at.heads // 2
+    span_values(span, v_span)
+    at.score(0, 0, span[:, :HD], at.causal())
+
+    @pl.loop(0, pairs)
+    def _(pair):
+        at.two_heads(pair, span[:, :HD], v_span[...], True, at.causal())
+
+    @pl.loop(0, QUARTERS)
+    def _(b):
+        values, ones = value_block(kv[2 * b + 1], tab[9, 0])
+        v_block[:, :HD] = values
+        v_block[:, HD:] = ones
+        at.score(0, 0, kv[2 * b])
+
+        @pl.loop(0, pairs)
+        def _(pair):
+            at.two_heads(pair, kv[2 * b], v_block[...])
+
+    at.finish()
+
+
+def attend(table, queries, span, kv):
+    rows, width = queries.shape
     vmem = pl.BlockSpec(memory_space=pltpu.VMEM)
     smem = pl.BlockSpec(memory_space=pltpu.SMEM)
     return pl.pallas_call(
-        functools.partial(attend_kernel, heads, span),
-        out_shape=jax.ShapeDtypeStruct((span, width), jnp.bfloat16),
-        in_specs=[smem, vmem, vmem, vmem, vmem],
+        attend_kernel,
+        out_shape=jax.ShapeDtypeStruct((rows, width), jnp.bfloat16),
+        in_specs=[smem, vmem, vmem, vmem],
         out_specs=vmem,
         scratch_shapes=[
-            pltpu.VMEM((cached + span, HD), jnp.bfloat16),
-            pltpu.VMEM((cached + span, 2 * HD), jnp.bfloat16),
-            pltpu.VMEM((2, QT, cached + span), jnp.float32),
-            pltpu.VMEM((2, QT, HD), jnp.float32),
-            pltpu.VMEM((QT, 2 * HD), jnp.float32),
+            pltpu.VMEM((rows, 2 * HD), jnp.bfloat16),
+            pltpu.VMEM((BLOCK, 2 * HD), jnp.bfloat16),
+            attention_scratch(rows, width),
         ],
         compiler_params=pltpu.CompilerParams(vmem_limit_bytes=48 * 1024 * 1024),
-        cost_estimate=pl.CostEstimate(
-            flops=4 * span * width * cached, bytes_accessed=8 * 1024 * 1024, transcendentals=span * heads * cached
-        ),
-    )(table, queries, span_kv, keys, values)
-
-
-def dense_exchange(table, dest, span, pool, slots, flags):
+    )(table, queries, span, kv)
+
+
+def dense(table, dest, queries, span, pool, slots, flags):
     tp_size, dec_size = lax.axis_size("tp"), lax.axis_size("dec")
     devices = tp_size * dec_size
     width = span.shape[1]
@@ -592,26 +653,26 @@
     fetched = lax.all_to_all(view[asked, :, source_rows], axes, split_axis=0, concat_axis=0, tiled=True)
     live_index, live_count = compact_slots(flags)
     live_index = jnp.where(jnp.arange(CTXP) < live_count, live_index, live_index[0])
-    cached = fetched.reshape(devices, PAGE, width)[live_index].reshape(CTXP, 2, 2, 32, 2, HD)
-    cached = jnp.transpose(cached, (4, 2, 1, 0, 3, 5)).reshape(2, CTXP * PAGE, HD)
+    cached = fetched.reshape(devices, PAGE, width)[live_index]
+    cached = cached.reshape(CTXP, 2, QUARTERS, ROWS, 2, HD)
+    cached = jnp.transpose(cached, (2, 4, 1, 0, 3, 5)).reshape(NCH, BLOCK, HD)
     new_pages = span.reshape(-1, PAGE, width)
     chosen = (dest[None, :] == jnp.arange(dec_size, dtype=jnp.int32)[:, None]).astype(jnp.bfloat16)
     outgoing = jnp.einsum("dp,pkc->dkc", chosen, new_pages, preferred_element_type=jnp.float32).astype(jnp.bfloat16)
     placed = lax.all_to_all(outgoing, "dec", split_axis=0, concat_axis=0, tiled=True)
     placed = lax.all_to_all(placed, "tp", split_axis=0, concat_axis=2, tiled=True)
-    return (cached[0], cached[1], placed)
+    return (attend(table, queries, span, cached), placed)
 
 
 def body(queries, span_kv, page_pool, cache_slot, cache_live, span_dest):
     table = make_table(cache_slot, cache_live)
-    keys, values, placed = lax.cond(
+    attn_out, placed = lax.cond(
         table[10, 0] > 0,
-        lambda tab, dest, span, pool, slots, flags: dense_exchange(tab, dest, span, pool, slots, flags),
-        lambda tab, dest, span, pool, slots, flags: tuple(exchange(tab, dest, span, pool)),
-        table, span_dest[0], span_kv[0], page_pool, cache_slot[0], cache_live[0],
+        lambda *a: dense(*a),
+        lambda tab, dest, q, span, pool, slots, flags: tuple(fused(tab, dest, q, span, pool)),
+        table, span_dest[0], queries[0], span_kv[0], page_pool, cache_slot[0], cache_live[0],
     )
-    attn_out = attend(queries[0], span_kv[0], table, keys, values)[None]
-    return (attn_out, placed)
+    return (attn_out[None], placed)
 
 
 def solution(mesh):

time: 207 us -> 137 us (0.66)
  the two profiles are of different devices: /device:TPU:1 before, /device:TPU:33 now
where the time goes in v3:
time: 137 us
  Pallas kernels  130 us (95%)
  local copies, waits for them, and re-layouts  4.75 us (3%)
    pallas_call x1, Pallas kernels, fused(): pl.pallas_call(fused_kernel, out_shape=[jax.ShapeDtypeStruct((rows, width...  121 us
    pallas_call x1, Pallas kernels, make_table(): pl.pallas_call(table_kernel, out_shape=jax.ShapeDtypeStruct((LISTS, 128),...  9.13 us
    unnamed x2, local copies, waits for them, and re-layouts  3.64 us

profile of v3, /device:TPU:33, one launch (start us, length us, event | category | flops | bytes accessed | tf_op | source)
XLA Modules:
  0.0 137.1 jit_solution(14621028164825415960)
XLA Ops:
  0.6 0.7 fusion.6
  1.3 0.6 broadcast_in_dim.41.row_ref
  1.9 9.1 %shard_map.77 = s32[16,128]{1,0:T(8,128)S(1)} custom-call(s32[8,128]{1,0:T(8,128)} %broadcast_in_dim.41.row_ref), custom_call_target="tpu_custom_call" | custom-call | tf_op jit(solution)/shard_map/pallas_call | solution.py:160
  11.0 0.5 slice.6
  12.2 121.2 %conditional.1 = (bf16[2,128,2048]{2,1,0:T(8,128)(2,1)S(1)}, bf16[768,1024]{1,0:T(8,128)(2,1)}) conditional(s32[]{:T(128)} %bitcast.21, (s32[1,6]{1,0:T(1,128)}, s32[16,128]{1,0:T(8,128)S(1)}, bf16[768,1024]{1,0:T(8,128)(2,1)}, bf16[768,256]{1,0:T(8,128)(2,1)}, bf16[8,128,2048]{2,1,0:T(8,128)(2,1)}) %tuple.35, (s32[1,6]{1,0:T(1,128)}, ...), branch_computations={%region_0.1_spmd, %region_1.5_spmd} | conditional | flops 6854751 | bytes 90202736 | solution.py:669
  12.2 121.0 %branch_0_fun.1 = (bf16[768,1024]{1,0:T(8,128)(2,1)}, bf16[2,128,2048]{2,1,0:T(8,128)(2,1)S(1)}) custom-call(s32[16,128]{1,0:T(8,128)S(1)} %get-tuple-element.32.tab, s32[6]{0:T(128)} %bitcast.51, bf16[768,1024]{1,0:T(8,128)(2,1)} %get-tuple-element.34.q, bf16[768,256]{1,0:T(8,128)(2,1)} %get-tuple-element.35.span, bf16[8,128,2048]{2,1,0:T(8,128)(2,1)} %get-tuple-element.36.pool), custom_call_target="tpu_custom_call" | custom-call | tf_op jit(solution)/shard_map/cond/branch_0_fun/pallas_call | solution.py:584
  133.4 2.7 %copy.74 = bf16[1,768,1024]{2,1,0:T(8,128)(2,1)} copy(bf16[1,768,1024]{2,1,0:T(8,128)(2,1)} %bitcast.24) | data formatting | bytes 3145728
  136.1 1.0 copy.75

commit v4 on v3

--- a/solution.py
+++ b/solution.py
@@ -181,7 +181,7 @@
     def __init__(self, tab, pool, span, pages, kv, refs, sems):
         self.tab, self.pool, self.span, self.pages, self.kv = tab, pool, span, pages, kv
         (self.pool16, self.send_y, self.recv_y, self.send_z, self.recv_z, self.send_x, self.recv_x, self.send_c,
-         self.span_pad, self.send_d) = refs
+         self.span_pad, self.send_n, self.recv_n) = refs
         self.sems = sems
         self.t, self.d, self.y, self.z, self.x, self.core = coords()
 
@@ -191,15 +191,17 @@
         for device in [self.peer("c", 1)] + [self.peer(a, k) for a in "yzx" for k in (1, 2, 3)]:
             pl.semaphore_signal(sem, inc=1, device_id=device, device_id_type=MESH)
 
+        zlo = self.z % 2
+
         @pl.loop(0, 16)
         def _(n):
-            ot, od = n // 2, t * 2 + n % 2
-
-            @pl.when((ot != t) | (od != d))
+            device = {"tp": n // 2, "dec": self.x * 4 + (t % 2) * 2 + n % 2}
+
+            @pl.when((n // 2 != t) | (device["dec"] != d))
             def _():
-                pl.semaphore_signal(sem, inc=1, device_id={"tp": ot, "dec": od}, device_id_type=MESH)
-
-        pl.semaphore_wait(sem, 26 - jnp.where(d // 2 == t, 1, 0))
+                pl.semaphore_signal(sem, inc=1, device_id=device, device_id_type=MESH)
+
+        pl.semaphore_wait(sem, 26 - jnp.where(t % 2 == zlo, 1, 0))
 
     def peer(self, axis, k):
         t, d, y, z, x, c = self.t, self.d, self.y, self.z, self.x, self.core
@@ -236,7 +238,6 @@
 
     def start_pool(self):
         for half in range(QUARTERS):
-            self.pool_own(half).start()
             self.pool_pair(half, self.core).start()
 
     def wait_pool(self, half):
@@ -268,7 +269,7 @@
     def pack_y(self, ch):
         half, kv = ch // 2, ch % 2
 
-        @pl.loop(0, CAP_Y)
+        @pl.loop(0, CAP_Y, unroll=True)
         def _(n):
             slot = self.tab[0, n]
             for k in range(4):
@@ -286,7 +287,7 @@
     def pack_z(self, ch):
         self.wait_hop("y", ch)
 
-        @pl.loop(0, CAP_Z)
+        @pl.loop(0, CAP_Z, unroll=True)
         def _(n):
             for k in range(4):
                 to = (self.z + k) % 4
@@ -301,7 +302,7 @@
     def pack_x(self, ch):
         self.wait_hop("z", ch)
 
-        @pl.loop(0, CAP_X)
+        @pl.loop(0, CAP_X, unroll=True)
         def _(n):
             for k in range(4):
                 to = (self.x + k) % 4
@@ -325,7 +326,7 @@
     def pack_c(self, ch):
         self.wait_hop("x", ch)
 
-        @pl.loop(0, CTXP)
+        @pl.loop(0, CTXP, unroll=True)
         def _(n):
             rows = pl.ds(pl.multiple_of(n * ROWS, ROWS), ROWS)
             own = pl.ds(pl.multiple_of((self.core * CTXP + n) * ROWS, ROWS), ROWS)
@@ -337,66 +338,81 @@
     def wait_last(self, ch):
         self.last(ch, 1 - self.core).wait_recv()
 
-    def new_page(self, n, ot, od, half, t):
-        cols = pl.ds(pl.multiple_of(t * 256, 256), 256)
+    def new_hop(self, k, source):
         return self.remote(
-            self.send_d.at[n],
-            self.pages.at[half, :, cols],
-            self.sems["new_send"].at[n],
-            self.sems["new_recv"].at[half * 8 + t],
-            {"tp": ot, "dec": od},
-        )
-
-    def own_page(self):
-        cols = pl.ds(pl.multiple_of(self.t * 256, 256), 256)
-        return pltpu.make_async_copy(
-            self.send_d.at[self.d], self.pages.at[self.d % 2, :, cols], self.sems["new_send"].at[self.d]
+            self.send_n.at[k - 1],
+            self.recv_n.at[source],
+            self.sems["new_send"].at[k - 1],
+            self.sems["new_recv"].at[k - 1],
+            self.peer("x", k),
         )
 
     def start_new(self, dest):
         self.span_pad[0:6] = self.span[...].reshape(6, PAGE, 256)
         self.span_pad[6] = jnp.zeros((PAGE, 256), jnp.bfloat16)
-        ot = self.d // 2
-
+        for k in range(4):
+            for j in range(4):
+                column = ((self.x + k) % 4) * 4 + j
+                page = jnp.int32(6)
+                for p in range(6):
+                    page = jnp.where(dest[p] == column, p, page)
+                if k == 0:
+                    self.recv_n[self.x, j] = self.span_pad[page]
+                else:
+                    self.send_n[k - 1, j] = self.span_pad[page]
+        for k in (1, 2, 3):
+            self.new_hop(k, self.x).start()
+
+    def new_page(self, n, owner_t, owner_d, core, t):
+        cols = pl.ds(pl.multiple_of(t * 256, 256), 256)
+        return self.remote(
+            self.recv_n.at[n // 4, n % 4],
+            self.pages.at[core, :, cols],
+            self.sems["page_send"].at[n],
+            self.sems["page_recv"].at[core * 8 + t],
+            {"tp": owner_t, "dec": owner_d},
+        )
+
+    def own_page(self, n):
+        cols = pl.ds(pl.multiple_of(self.t * 256, 256), 256)
+        return pltpu.make_async_copy(
+            self.recv_n.at[n // 4, n % 4], self.pages.at[self.core, :, cols], self.sems["page_send"].at[n]
+        )
+
+    def each_page(self, mine, other):
         @pl.loop(0, 16)
         def _(n):
-            od = (self.d + n) % 16
-            page = jnp.int32(6)
-            for p in range(6):
-                page = jnp.where(dest[p] == od, p, page)
-            self.send_d[od] = self.span_pad[page]
-            own = (ot == self.t) & (od == self.d)
+            owner_t, owner_d = (n // 4) * 2 + self.z % 2, self.x * 4 + n % 4
+            own = (owner_t == self.t) & (owner_d == self.d)
 
             @pl.when(own)
             def _():
-                self.own_page().start()
+                mine(self.own_page(n))
 
             @pl.when(jnp.logical_not(own))
             def _():
-                self.new_page(od, ot, od, self.d % 2, self.t).start()
+                other(self.new_page(n, owner_t, owner_d, self.core, self.t))
+
+    def forward_new(self):
+        for k in (1, 2, 3):
+            self.new_hop(k, (self.x + 4 - k) % 4).wait_recv()
+        self.each_page(lambda copy: copy.start(), lambda copy: copy.start())
 
     def wait_new(self):
-        t, d = self.t, self.d
+        self.each_page(lambda copy: copy.wait(), lambda copy: copy.wait_send())
+        block = (self.t // 2) * 4 + self.d % 4
 
         @pl.loop(0, 16)
         def _(n):
-            st, half = n // 2, n % 2
-            sd = t * 2 + half
-            own = (st == t) & (sd == d)
-
-            @pl.when(own)
+            sender_t, core = n // 2, n % 2
+            sender_d = self.x * 4 + (self.t % 2) * 2 + core
+
+            @pl.when((sender_t != self.t) | (sender_d != self.d))
             def _():
-                self.own_page().wait()
-
-            @pl.when(jnp.logical_not(own))
-            def _():
-                self.new_page(d, st, sd, half, st).wait_recv()
-
-        @pl.loop(0, 16)
-        def _(n):
-            @pl.when((d // 2 != t) | (n != d))
-            def _():
-                self.new_page(n, d // 2, n, d % 2, t).wait_send()
+                self.new_page(block, sender_t, sender_d, core, sender_t).wait_recv()
+
+        for k in (1, 2, 3):
+            self.new_hop(k, self.x).wait_send()
 
     def wait_sends(self):
         for half in range(QUARTERS):
@@ -421,12 +437,13 @@
         [vmem((4 * CAP_X,) + unit, bf16) for _ in range(NCH)],
         vmem((NCH, CTXP * ROWS, HD), bf16),
         vmem((7, PAGE, 256), bf16),
-        vmem((16, PAGE, 256), bf16),
+        vmem((3, 4, PAGE, 256), bf16),
+        vmem((4, 4, PAGE, 256), bf16),
     ]
     sems = {
         "own": dma((QUARTERS,)), "pair_send": dma((QUARTERS,)), "pair_recv": dma((QUARTERS,)), "send": dma((3, NCH, 3)),
-        "recv": dma((3, NCH, 3)), "last_send": dma((NCH,)), "last_recv": dma((NCH,)), "new_send": dma((16,)),
-        "new_recv": dma((16,)),
+        "recv": dma((3, NCH, 3)), "last_send": dma((NCH,)), "last_recv": dma((NCH,)), "new_send": dma((3,)),
+        "new_recv": dma((3,)), "page_send": dma((16,)), "page_recv": dma((16,)),
     }
     return refs, sems
 
@@ -516,38 +533,47 @@
     v_span[:, HD:] = jnp.ones((v_span.shape[0], HD), jnp.bfloat16)
 
 
+FORWARD = 10
+
+
 def fused_kernel(tab, dest, q, span, pool, out, pages, kv, v_span, v_block, attn, refs, sems):
     ex = Exchange(tab, pool, span, pages, kv, refs, sems)
     at = Attention(q, out, *attn)
     pairs = at.heads // 2
-    first_block = 8
-
+    first_block = 10
+
+    for quarter in range(QUARTERS):
+        ex.pool_own(quarter).start()
     ex.barrier()
     ex.start_pool()
+    ex.wait_pool(0)
+    ex.pack_y(0)
+    ex.pack_y(1)
+    ex.start_new(dest)
     span_values(span, v_span)
     at.score(0, 0, span[:, :HD], at.causal())
 
     @pl.loop(0, first_block + QUARTERS * pairs)
     def _(step):
-        for i in range(NCH + 3):
+        for i in range(1, NCH + 3):
 
             @pl.when(step == 2 * i)
             def _(i=i):
-                if i == 0:
-                    ex.wait_pool(0)
-                    ex.pack_y(0)
-                if 0 <= i - 3 < NCH:
-                    ex.pack_c(i - 3)
-                if 0 <= i - 2 < NCH:
-                    ex.pack_x(i - 2)
-                if 0 <= i - 1 < NCH:
+                if i - 1 < NCH:
                     ex.pack_z(i - 1)
                 if i + 1 < NCH:
                     if i % 2 == 1:
                         ex.wait_pool((i + 1) // 2)
                     ex.pack_y(i + 1)
-                if i == NCH:
-                    ex.start_new(dest)
+                if i == FORWARD:
+                    ex.forward_new()
+
+            @pl.when(step == 2 * i + 1)
+            def _(i=i):
+                if 0 <= i - 2 < NCH:
+                    ex.pack_x(i - 2)
+                if 0 <= i - 3 < NCH:
+                    ex.pack_c(i - 3)
 
         @pl.when(step < pairs)
         def _():

time: 137 us -> 110 us (0.80)
  the two profiles are of different devices: /device:TPU:33 before, /device:TPU:1 now
where the time goes in v4:
time: 110 us
  Pallas kernels  103 us (94%)
  local copies, waits for them, and re-layouts  4.75 us (4%)
  between operations  1.3 us (1%)
    pallas_call x1, Pallas kernels, fused(): pl.pallas_call(fused_kernel, out_shape=[jax.ShapeDtypeStruct((rows, width...  92.5 us
    pallas_call x1, Pallas kernels, make_table(): pl.pallas_call(table_kernel, out_shape=jax.ShapeDtypeStruct((LISTS, 128),...  10.3 us
    unnamed x2, local copies, waits for them, and re-layouts  3.64 us

profile of v4, /device:TPU:1, one launch (start us, length us, event | category | flops | bytes accessed | tf_op | source)
XLA Modules:
  0.0 109.7 jit_solution(6544673469471823745)
XLA Ops:
  0.6 0.7 fusion.6
  1.3 0.6 broadcast_in_dim.41.row_ref
  1.9 10.3 %shard_map.77 = s32[16,128]{1,0:T(8,128)S(1)} custom-call(s32[8,128]{1,0:T(8,128)} %broadcast_in_dim.41.row_ref), custom_call_target="tpu_custom_call" | custom-call | tf_op jit(solution)/shard_map/pallas_call | solution.py:160
  12.2 0.5 slice.6
  13.4 92.7 %conditional.1 = (bf16[2,128,2048]{2,1,0:T(8,128)(2,1)S(1)}, bf16[768,1024]{1,0:T(8,128)(2,1)}) conditional(s32[]{:T(128)} %bitcast.21, (s32[1,6]{1,0:T(1,128)}, s32[16,128]{1,0:T(8,128)S(1)}, bf16[768,1024]{1,0:T(8,128)(2,1)}, bf16[768,256]{1,0:T(8,128)(2,1)}, bf16[8,128,2048]{2,1,0:T(8,128)(2,1)}) %tuple.35, (s32[1,6]{1,0:T(1,128)}, ...), branch_computations={%region_0.1_spmd, %region_1.5_spmd} | conditional | flops 6854751 | bytes 90202736 | solution.py:695
  13.4 92.5 %branch_0_fun.1 = (bf16[768,1024]{1,0:T(8,128)(2,1)}, bf16[2,128,2048]{2,1,0:T(8,128)(2,1)S(1)}) custom-call(s32[16,128]{1,0:T(8,128)S(1)} %get-tuple-element.32.tab, s32[6]{0:T(128)} %bitcast.51, bf16[768,1024]{1,0:T(8,128)(2,1)} %get-tuple-element.34.q, bf16[768,256]{1,0:T(8,128)(2,1)} %get-tuple-element.35.span, bf16[8,128,2048]{2,1,0:T(8,128)(2,1)} %get-tuple-element.36.pool), custom_call_target="tpu_custom_call" | custom-call | tf_op jit(solution)/shard_map/cond/branch_0_fun/pallas_call | solution.py:610
  106.1 2.7 %copy.74 = bf16[1,768,1024]{2,1,0:T(8,128)(2,1)} copy(bf16[1,768,1024]{2,1,0:T(8,128)(2,1)} %bitcast.24) | data formatting | bytes 3145728
  108.8 1.0 copy.75

commit v5 on v4

--- a/solution.py
+++ b/solution.py
@@ -448,9 +448,12 @@
     return refs, sems
 
 
+ONES = 16
+
+
 class Attention:
-    def __init__(self, q, out, s, mx, m, acc):
-        self.q, self.out, self.s, self.mx, self.m, self.acc = q, out, s, mx, m, acc
+    def __init__(self, q, s, mx, m, acc):
+        self.q, self.s, self.mx, self.m, self.acc = q, s, mx, m, acc
         self.span = q.shape[0]
         self.heads = q.shape[1] // HD
         self.coef = LOG2E / math.sqrt(HD)
@@ -458,87 +461,106 @@
     def columns(self, n):
         return pl.ds(pl.multiple_of(n * HD, HD), HD)
 
-    def score(self, n, slot, k, mask=None):
+    def product(self, k, q):
+        return lax.dot_general(k, q, (((1,), (1,)), ((), ())), preferred_element_type=jnp.float32)
+
+    def fold(self, part):
+        return jnp.max(part.reshape(part.shape[0] // 8, 8, part.shape[1]), axis=0)
+
+    def weights(self, part, top):
+        return jnp.exp2((part - top) * self.coef).astype(jnp.bfloat16)
+
+    def score(self, n, slot, k):
         q = self.q[:, self.columns(n)]
-        width = k.shape[0]
-        step = min(512, width)
         top = None
-        for start in range(0, width, step):
-            size = min(step, width - start)
-            part = lax.dot_general(
-                q, k[start : start + size], (((1,), (1,)), ((), ())), preferred_element_type=jnp.float32
-            )
-            if mask is not None:
-                part = jnp.where(mask[:, start : start + size], part, NEG)
-            self.s[slot][:, start : start + size] = part
-            for c in range(0, size, HD):
-                piece = part[:, c : c + HD]
-                top = piece if top is None else jnp.maximum(top, piece)
+        for start in range(0, BLOCK, KEYS):
+            part = self.product(k[start : start + KEYS], q)
+            self.s[slot][start : start + KEYS, :] = part
+            piece = self.fold(part)
+            top = piece if top is None else jnp.maximum(top, piece)
         self.mx[slot][...] = top
 
-    def mix(self, n, slot, v, first):
-        top = jnp.broadcast_to(jnp.max(self.mx[slot][...], axis=1, keepdims=True), (self.span, HD))
-        if not first:
-            old = self.m[n]
-            top = jnp.maximum(old, top)
-            fade = jnp.exp2((old - top) * self.coef)
-        self.m[n] = top
-        weights = [
-            jnp.exp2((self.s[slot][:, c : c + HD] - top) * self.coef).astype(jnp.bfloat16)
-            for c in range(0, v.shape[0], HD)
-        ]
-        mixed = jnp.dot(jnp.concatenate(weights, axis=1), v, preferred_element_type=jnp.float32)
-        if not first:
-            mixed += self.acc[n] * jnp.concatenate([fade, fade], axis=1)
-        self.acc[n] = mixed
-
-    def two_heads(self, pair, k, v, first=False, mask=None):
+    def mix(self, n, slot, vt):
+        top = jnp.max(self.mx[slot][...], axis=0, keepdims=True)
+        old = self.m[n, 0:1, :]
+        top = jnp.maximum(old, top)
+        fade = jnp.exp2((old - top) * self.coef)
+        self.m[n] = jnp.broadcast_to(top, (8, self.span))
+        weights = [self.weights(self.s[slot][start : start + KEYS, :], top) for start in range(0, BLOCK, KEYS)]
+        mixed = jnp.dot(vt[...], jnp.concatenate(weights, axis=0), preferred_element_type=jnp.float32)
+        self.acc[n] = self.acc[n] * fade + mixed
+
+    def score_span(self, n, slot, k):
+        q = self.q[:, self.columns(n)]
+        shape = (KEYS, KEYS)
+        diagonal = lax.broadcasted_iota(jnp.int32, shape, 0) <= lax.broadcasted_iota(jnp.int32, shape, 1)
+        top = None
+        for start in range(0, self.span, KEYS):
+            part = self.product(k[start : start + KEYS], q[start:])
+            edge = jnp.where(diagonal, part[:, :KEYS], NEG)
+            part = edge if start + KEYS == self.span else jnp.concatenate([edge, part[:, KEYS:]], axis=1)
+            self.s[slot][start : start + KEYS, start:] = part
+            piece = self.fold(part)
+            if start:
+                piece = jnp.concatenate([top[:, :start], jnp.maximum(top[:, start:], piece)], axis=1)
+            top = piece
+        self.mx[slot][...] = top
+
+    def mix_span(self, n, slot, vt):
+        top = jnp.max(self.mx[slot][...], axis=0, keepdims=True)
+        self.m[n] = jnp.broadcast_to(top, (8, self.span))
+        for start in range(0, self.span, KEYS):
+            weights = self.weights(self.s[slot][start : start + KEYS, start:], top[:, start:])
+            mixed = jnp.dot(vt[:, start : start + KEYS], weights, preferred_element_type=jnp.float32)
+            if start:
+                self.acc[n, :, start:] += mixed
+            else:
+                self.acc[n] = mixed
+
+    def two_heads(self, pair, score, mix, k, v):
         n = pair * 2
-        self.score(n + 1, 1, k, mask)
-        self.mix(n, 0, v, first)
-        self.score(jnp.minimum(n + 2, self.heads - 1), 0, k, mask)
-        self.mix(n + 1, 1, v, first)
-
-    def causal(self):
-        shape = (self.span, self.span)
-        return lax.broadcasted_iota(jnp.int32, shape, 1) <= lax.broadcasted_iota(jnp.int32, shape, 0)
-
-    def finish(self):
-        @pl.loop(0, self.heads)
-        def _(n):
-            acc = self.acc[n]
-            self.out[:, self.columns(n)] = (acc[:, :HD] / acc[:, HD:]).astype(self.out.dtype)
+        score(n + 1, 1, k)
+        mix(n, 0, v)
+        score(jnp.minimum(n + 2, self.heads - 1), 0, k)
+        mix(n + 1, 1, v)
+
+    def result(self, n):
+        acc = self.acc[n]
+        return jnp.transpose((acc[:HD] / acc[HD : HD + 1]).astype(jnp.bfloat16))
+
+
+KEYS = 256
 
 
 def attention_scratch(span, width):
     heads = width // HD
-    wide = max(BLOCK, span)
     f32 = jnp.float32
     return [
-        [pltpu.VMEM((span, wide), f32) for _ in range(2)],
-        [pltpu.VMEM((span, HD), f32) for _ in range(2)],
-        pltpu.VMEM((heads, span, HD), f32),
-        pltpu.VMEM((heads, span, 2 * HD), f32),
+        [pltpu.VMEM((BLOCK, span), f32) for _ in range(2)],
+        [pltpu.VMEM((8, span), f32) for _ in range(2)],
+        pltpu.VMEM((heads, 8, span), f32),
+        pltpu.VMEM((heads, HD + ONES, span), f32),
     ]
 
 
-def value_block(values, live):
-    row = lax.broadcasted_iota(jnp.int32, (BLOCK, HD), 0) % (CTXP * ROWS)
-    used = row < live * ROWS
-    return jnp.where(used, values, 0).astype(jnp.bfloat16), jnp.where(used, 1.0, 0.0).astype(jnp.bfloat16)
-
-
 def span_values(span_ref, v_span):
-    v_span[:, :HD] = span_ref[:, HD:]
-    v_span[:, HD:] = jnp.ones((v_span.shape[0], HD), jnp.bfloat16)
-
-
-FORWARD = 10
-
-
-def fused_kernel(tab, dest, q, span, pool, out, pages, kv, v_span, v_block, attn, refs, sems):
+    v_span[:HD, :] = jnp.transpose(span_ref[:, HD:])
+    v_span[HD:, :] = jnp.ones((ONES, v_span.shape[1]), jnp.bfloat16)
+
+
+def block_values(values, live, v_block):
+    key = lax.broadcasted_iota(jnp.int32, (HD, BLOCK), 1) % (CTXP * ROWS)
+    used = key < live * ROWS
+    v_block[:HD, :] = jnp.where(used, jnp.transpose(values), 0).astype(jnp.bfloat16)
+    v_block[HD:, :] = jnp.where(used[:ONES], 1.0, 0.0).astype(jnp.bfloat16)
+
+
+FORWARD = 9
+
+
+def fused_kernel(tab, dest, q, span, pool, out, pages, kv, v_span, v_block, done, done_sem, attn, refs, sems):
     ex = Exchange(tab, pool, span, pages, kv, refs, sems)
-    at = Attention(q, out, *attn)
+    at = Attention(q, *attn)
     pairs = at.heads // 2
     first_block = 10
 
@@ -551,7 +573,11 @@
     ex.pack_y(1)
     ex.start_new(dest)
     span_values(span, v_span)
-    at.score(0, 0, span[:, :HD], at.causal())
+    at.score_span(0, 0, span[:, :HD])
+
+    def write_out(pair):
+        cols = pl.ds(pl.multiple_of(pair * 2 * HD, 2 * HD), 2 * HD)
+        return pltpu.make_async_copy(done.at[:, cols], out.at[:, cols], done_sem.at[pair])
 
     @pl.loop(0, first_block + QUARTERS * pairs)
     def _(step):
@@ -577,7 +603,7 @@
 
         @pl.when(step < pairs)
         def _():
-            at.two_heads(step, span[:, :HD], v_span[...], True, at.causal())
+            at.two_heads(step, at.score_span, at.mix_span, span[:, :HD], v_span)
 
         for b in range(QUARTERS):
 
@@ -585,19 +611,28 @@
             def _(b=b):
                 ex.wait_last(2 * b)
                 ex.wait_last(2 * b + 1)
-                values, ones = value_block(kv[2 * b + 1], tab[9, 0])
-                v_block[:, :HD] = values
-                v_block[:, HD:] = ones
+                block_values(kv[2 * b + 1], tab[9, 0], v_block)
                 at.score(0, 0, kv[2 * b])
 
         @pl.when(step >= first_block)
         def _():
             e = step - first_block
-            at.two_heads(e % pairs, kv[(e // pairs) * 2], v_block[...])
-
-    at.finish()
+            at.two_heads(e % pairs, at.score, at.mix, kv[(e // pairs) * 2], v_block)
+
+        @pl.when(step >= first_block + (QUARTERS - 1) * pairs)
+        def _():
+            pair = (step - first_block) % pairs
+            for n in range(2):
+                done[:, at.columns(pair * 2 + n)] = at.result(pair * 2 + n)
+            write_out(pair).start()
+
+    for pair in range(pairs):
+        write_out(pair).wait()
     ex.wait_new()
     ex.wait_sends()
+
+
+VMEM_MIB = 56
 
 
 def fused(table, dest, queries, span, pool):
@@ -611,43 +646,45 @@
         fused_kernel,
         out_shape=[jax.ShapeDtypeStruct((rows, width), bf16), jax.ShapeDtypeStruct((2, PAGE, 2048), bf16)],
         in_specs=[smem, smem, vmem, vmem, hbm],
-        out_specs=[vmem, hbm],
+        out_specs=[hbm, hbm],
         scratch_shapes=[
             pltpu.VMEM((NCH, BLOCK, HD), bf16),
-            pltpu.VMEM((rows, 2 * HD), bf16),
-            pltpu.VMEM((BLOCK, 2 * HD), bf16),
+            pltpu.VMEM((HD + ONES, rows), bf16),
+            pltpu.VMEM((HD + ONES, BLOCK), bf16),
+            pltpu.VMEM((rows, width), bf16),
+            pltpu.SemaphoreType.DMA((width // HD // 2,)),
             attention_scratch(rows, width),
             refs,
             sems,
         ],
         compiler_params=pltpu.CompilerParams(
-            collective_id=1, has_side_effects=True, vmem_limit_bytes=62 * 1024 * 1024
+            collective_id=1, has_side_effects=True, vmem_limit_bytes=VMEM_MIB * 1024 * 1024
         ),
     )(table, dest, queries, span, pool)
 
 
 def attend_kernel(tab, q, span, kv, out, v_span, v_block, attn):
-    at = Attention(q, out, *attn)
+    at = Attention(q, *attn)
     pairs = at.heads // 2
     span_values(span, v_span)
-    at.score(0, 0, span[:, :HD], at.causal())
+    at.score_span(0, 0, span[:, :HD])
 
     @pl.loop(0, pairs)
     def _(pair):
-        at.two_heads(pair, span[:, :HD], v_span[...], True, at.causal())
+        at.two_heads(pair, at.score_span, at.mix_span, span[:, :HD], v_span)
 
     @pl.loop(0, QUARTERS)
     def _(b):
-        values, ones = value_block(kv[2 * b + 1], tab[9, 0])
-        v_block[:, :HD] = values
-        v_block[:, HD:] = ones
+        block_values(kv[2 * b + 1], tab[9, 0], v_block)
         at.score(0, 0, kv[2 * b])
 
         @pl.loop(0, pairs)
         def _(pair):
-            at.two_heads(pair, kv[2 * b], v_block[...])
-
-    at.finish()
+            at.two_heads(pair, at.score, at.mix, kv[2 * b], v_block)
+
+    @pl.loop(0, at.heads)
+    def _(n):
+        out[:, at.columns(n)] = at.result(n)
 
 
 def attend(table, queries, span, kv):
@@ -660,8 +697,8 @@
         in_specs=[smem, vmem, vmem, vmem],
         out_specs=vmem,
         scratch_shapes=[
-            pltpu.VMEM((rows, 2 * HD), jnp.bfloat16),
-            pltpu.VMEM((BLOCK, 2 * HD), jnp.bfloat16),
+            pltpu.VMEM((HD + ONES, rows), jnp.bfloat16),
+            pltpu.VMEM((HD + ONES, BLOCK), jnp.bfloat16),
             attention_scratch(rows, width),
         ],
         compiler_params=pltpu.CompilerParams(vmem_limit_bytes=48 * 1024 * 1024),

time: 110 us -> 101 us (0.918)
  Pallas kernels: 103 us -> 95.8 us
  local copies, waits for them, and re-layouts: 4.75 us -> 3.22 us
    pallas_call x1, Pallas kernels: 92.5 us -> 85.5 us  [fused(): pl.pallas_call(fused_kernel, out_shape=[jax.ShapeDtypeStruct((rows, width...]
    unnamed x2, local copies, waits for them, and re-layouts: 3.64 us -> 2.11 us
where the time goes in v5:
time: 101 us
  Pallas kernels  95.8 us (95%)
  local copies, waits for them, and re-layouts  3.22 us (3%)
  between operations  1.3 us (1%)
    pallas_call x1, Pallas kernels, fused(): pl.pallas_call(fused_kernel, out_shape=[jax.ShapeDtypeStruct((rows, width...  85.5 us
    pallas_call x1, Pallas kernels, make_table(): pl.pallas_call(table_kernel, out_shape=jax.ShapeDtypeStruct((LISTS, 128),...  10.3 us
    unnamed x2, local copies, waits for them, and re-layouts  2.11 us

profile of v5, /device:TPU:1, one launch (start us, length us, event | category | flops | bytes accessed | tf_op | source)
XLA Modules:
  0.0 101.2 jit_solution(18365231858741354306)
XLA Ops:
  0.6 0.7 fusion.6
  1.3 0.6 broadcast_in_dim.41.row_ref
  1.9 10.3 %shard_map.77 = s32[16,128]{1,0:T(8,128)S(1)} custom-call(s32[8,128]{1,0:T(8,128)} %broadcast_in_dim.41.row_ref), custom_call_target="tpu_custom_call" | custom-call | tf_op jit(solution)/shard_map/pallas_call | solution.py:160
  12.2 0.5 slice.6
  13.4 85.7 %conditional.1 = (bf16[2,128,2048]{2,1,0:T(8,128)(2,1)S(1)}, bf16[768,1024]{1,0:T(8,128)(2,1)S(1)}) conditional(s32[]{:T(128)} %bitcast.21, (s32[1,6]{1,0:T(1,128)}, s32[16,128]{1,0:T(8,128)S(1)}, bf16[768,1024]{1,0:T(8,128)(2,1)}, bf16[768,256]{1,0:T(8,128)(2,1)}, bf16[8,128,2048]{2,1,0:T(8,128)(2,1)}) %tuple.35, (s32[1,6]{1,0:T(1,128)}, ...), branch_computations={%region_0.1_spmd, %region_1.5_spmd} | conditional | flops 6854751 | bytes 90202736 | solution.py:732
  13.4 85.5 %branch_0_fun.1 = (bf16[768,1024]{1,0:T(8,128)(2,1)S(1)}, bf16[2,128,2048]{2,1,0:T(8,128)(2,1)S(1)}) custom-call(s32[16,128]{1,0:T(8,128)S(1)} %get-tuple-element.32.tab, s32[6]{0:T(128)} %bitcast.52, bf16[768,1024]{1,0:T(8,128)(2,1)} %get-tuple-element.34.q, bf16[768,256]{1,0:T(8,128)(2,1)} %get-tuple-element.35.span, ...), custom_call_target="tpu_custom_call" | custom-call | tf_op jit(solution)/shard_map/cond/branch_0_fun/pallas_call | solution.py:645
  99.1 1.1 %copy.74 = bf16[1,768,1024]{2,1,0:T(8,128)(2,1)} copy(bf16[1,768,1024]{2,1,0:T(8,128)(2,1)S(1)} %bitcast.50) | data formatting | bytes 3145728
  100.3 1.0 copy.75

commit v6 on v5

--- a/solution.py
+++ b/solution.py
@@ -27,7 +27,6 @@
 
 MESH = pl.DeviceIdType.MESH
 CAP_Y, CAP_Z, CAP_X = 13, 25, 26
-LISTS = 16
 
 
 def coords():
@@ -39,28 +38,8 @@
     return jnp.where(cond, 1.0, 0.0).astype(dtype)
 
 
-def table_kernel(row_ref, tab_ref, all_ref, send_sem, recv_sem):
+def route(packed):
     t, d, y, z, x, core = coords()
-    n = 16
-    barrier = pltpu.get_barrier_semaphore()
-    for k in range(1, n):
-        pl.semaphore_signal(barrier, inc=1, device_id={"dec": (d + k) % n}, device_id_type=MESH)
-    pl.semaphore_wait(barrier, n - 1)
-
-    def copy(k, slot):
-        return pltpu.make_async_remote_copy(
-            src_ref=row_ref,
-            dst_ref=all_ref.at[slot],
-            send_sem=send_sem.at[k],
-            recv_sem=recv_sem.at[slot],
-            device_id={"dec": (d + k) % n},
-            device_id_type=MESH,
-        )
-
-    for k in range(1, n):
-        copy(k, d).start()
-    all_ref[d] = row_ref[...]
-
     bf16, f32 = jnp.bfloat16, jnp.float32
     oi = lax.broadcasted_iota(jnp.int32, (128, 128), 0)
     oj = lax.broadcasted_iota(jnp.int32, (128, 128), 1)
@@ -69,9 +48,6 @@
     owner_groups = (lambda o: o >> 1, lambda o: o & 0x4E, lambda o: o & 0x0C, lambda o: o & 0)
     row_groups = (lambda g: g & 0, lambda g: g >> 3, lambda g: g & 14, lambda g: g)
 
-    for k in range(1, n):
-        copy(k, (d + n - k) % n).wait_recv()
-    packed = jnp.concatenate([all_ref[g, 0:1, :] for g in range(n)], axis=0)
     o = lax.broadcasted_iota(jnp.int32, (16, 128), 1)
     g = lax.broadcasted_iota(jnp.int32, (16, 128), 0)
     g_zlo = (g >> 1) & 1
@@ -114,9 +90,9 @@
     mine = [(want.astype(f32) > 0) & place for want, place in zip(wants, places)]
     values = (
         o_c * 8 + g,
-        o_y * CAP_Y + rank_y,
-        o_z * CAP_Z + rank_z,
-        o_x * CAP_X + ranks[2],
+        o_y * CAP_Y + jnp.minimum(rank_y, CAP_Y - 1),
+        o_z * CAP_Z + jnp.minimum(rank_z, CAP_Z - 1),
+        o_x * CAP_X + jnp.minimum(ranks[2], CAP_X - 1),
     )
     lists = (
         (range(8),),
@@ -146,29 +122,7 @@
         size = jnp.sum(flag(live & (g == (d // 2) * 2 + c))).astype(jnp.int32)
         table = jnp.where((lane == 7 + c) & (place >= size), table[0:1, :], table)
     table = jnp.where(lane == 9, held, table)
-    table = jnp.where(lane == 10, jnp.maximum(over, 0), table)
-    square = jnp.concatenate([table.astype(f32), jnp.zeros((128 - CTXP, 128), f32)], axis=0)
-    tab_ref[...] = jnp.transpose(square)[:LISTS, :].astype(jnp.int32)
-    for k in range(1, n):
-        copy(k, d).wait_send()
-
-
-def make_table(cache_slot, cache_live):
-    row = jnp.where(cache_live[0, :, 0] == 1, cache_slot[0, :, 0], -1)
-    row = jnp.broadcast_to(row[None, :], (8, 128))
-    vmem = pl.BlockSpec(memory_space=pltpu.VMEM)
-    return pl.pallas_call(
-        table_kernel,
-        out_shape=jax.ShapeDtypeStruct((LISTS, 128), jnp.int32),
-        in_specs=[vmem],
-        out_specs=vmem,
-        scratch_shapes=[
-            pltpu.VMEM((16, 8, 128), jnp.int32),
-            pltpu.SemaphoreType.DMA((16,)),
-            pltpu.SemaphoreType.DMA((16,)),
-        ],
-        compiler_params=pltpu.CompilerParams(collective_id=0, has_side_effects=True),
-    )(row)
+    return table, over
 
 
 QUARTERS = 4
@@ -181,7 +135,7 @@
     def __init__(self, tab, pool, span, pages, kv, refs, sems):
         self.tab, self.pool, self.span, self.pages, self.kv = tab, pool, span, pages, kv
         (self.pool16, self.send_y, self.recv_y, self.send_z, self.recv_z, self.send_x, self.recv_x, self.send_c,
-         self.span_pad, self.send_n, self.recv_n) = refs
+         self.span_pad, self.send_n, self.recv_n, self.row, self.rows) = refs
         self.sems = sems
         self.t, self.d, self.y, self.z, self.x, self.core = coords()
 
@@ -191,6 +145,8 @@
         for device in [self.peer("c", 1)] + [self.peer(a, k) for a in "yzx" for k in (1, 2, 3)]:
             pl.semaphore_signal(sem, inc=1, device_id=device, device_id_type=MESH)
 
+        for k in range(1, 16):
+            pl.semaphore_signal(sem, inc=1, device_id={"dec": (d + k) % 16}, device_id_type=MESH)
         zlo = self.z % 2
 
         @pl.loop(0, 16)
@@ -201,7 +157,10 @@
             def _():
                 pl.semaphore_signal(sem, inc=1, device_id=device, device_id_type=MESH)
 
-        pl.semaphore_wait(sem, 26 - jnp.where(t % 2 == zlo, 1, 0))
+        pl.semaphore_wait(sem, 41 - jnp.where(t % 2 == zlo, 1, 0))
+
+    def entry(self, place, column, size):
+        return jnp.minimum(jnp.maximum(self.tab[place, column], 0), size - 1)
 
     def peer(self, axis, k):
         t, d, y, z, x, c = self.t, self.d, self.y, self.z, self.x, self.core
@@ -220,6 +179,25 @@
             src_ref=src, dst_ref=dst, send_sem=send_sem, recv_sem=recv_sem, device_id=device, device_id_type=MESH
         )
 
+    def row_copy(self, k, slot):
+        return self.remote(
+            self.row,
+            self.rows.at[slot],
+            self.sems["row_send"].at[k],
+            self.sems["row_recv"].at[slot],
+            {"dec": (self.d + k) % 16},
+        )
+
+    def start_rows(self):
+        for k in range(1, 16):
+            self.row_copy(k, self.d).start()
+        self.rows[self.d] = self.row[...]
+
+    def wait_rows(self):
+        for k in range(1, 16):
+            self.row_copy(k, (self.d + 16 - k) % 16).wait_recv()
+        return jnp.concatenate([self.rows[g, 0:1, :] for g in range(16)], axis=0)
+
     def pool_own(self, half):
         rows = pl.ds(self.core * 64 + half * ROWS, ROWS)
         return pltpu.make_async_copy(
@@ -271,7 +249,7 @@
 
         @pl.loop(0, CAP_Y, unroll=True)
         def _(n):
-            slot = self.tab[0, n]
+            slot = self.entry(n, 0, 16)
             for k in range(4):
                 to = (self.y + k) % 4
                 for zhi in range(2):
@@ -291,7 +269,7 @@
         def _(n):
             for k in range(4):
                 to = (self.z + k) % 4
-                block = self.recv_y[ch][self.tab[1 + to % 2, n] * 2 + to // 2]
+                block = self.recv_y[ch][self.entry(n, 1 + to % 2, 4 * CAP_Y) * 2 + to // 2]
                 if k == 0:
                     self.recv_z[ch][self.z * CAP_Z + n] = block
                 else:
@@ -306,7 +284,7 @@
         def _(n):
             for k in range(4):
                 to = (self.x + k) % 4
-                block = self.recv_z[ch][self.tab[3 + to, n]]
+                block = self.recv_z[ch][self.entry(n, 3 + to, 4 * CAP_Z)]
                 if k == 0:
                     self.recv_x[ch][self.x * CAP_X + n] = block
                 else:
@@ -330,8 +308,8 @@
         def _(n):
             rows = pl.ds(pl.multiple_of(n * ROWS, ROWS), ROWS)
             own = pl.ds(pl.multiple_of((self.core * CTXP + n) * ROWS, ROWS), ROWS)
-            self.kv[ch, own, :] = self.recv_x[ch][self.tab[7 + self.core, n]]
-            self.send_c[ch, rows, :] = self.recv_x[ch][self.tab[8 - self.core, n]]
+            self.kv[ch, own, :] = self.recv_x[ch][self.entry(n, 7 + self.core, 4 * CAP_X)]
+            self.send_c[ch, rows, :] = self.recv_x[ch][self.entry(n, 8 - self.core, 4 * CAP_X)]
 
         self.last(ch, self.core).start()
 
@@ -415,6 +393,8 @@
             self.new_hop(k, self.x).wait_send()
 
     def wait_sends(self):
+        for k in range(1, 16):
+            self.row_copy(k, self.d).wait_send()
         for half in range(QUARTERS):
             self.pool_pair(half, self.core).wait_send()
         for ch in range(NCH):
@@ -439,11 +419,14 @@
         vmem((7, PAGE, 256), bf16),
         vmem((3, 4, PAGE, 256), bf16),
         vmem((4, 4, PAGE, 256), bf16),
+        vmem((8, 128), jnp.int32),
+        vmem((16, 8, 128), jnp.int32),
     ]
     sems = {
         "own": dma((QUARTERS,)), "pair_send": dma((QUARTERS,)), "pair_recv": dma((QUARTERS,)), "send": dma((3, NCH, 3)),
         "recv": dma((3, NCH, 3)), "last_send": dma((NCH,)), "last_recv": dma((NCH,)), "new_send": dma((3,)),
         "new_recv": dma((3,)), "page_send": dma((16,)), "page_recv": dma((16,)),
+        "row_send": dma((16,)), "row_recv": dma((16,)), "table": dma((1,)),
     }
     return refs, sems
 
@@ -558,7 +541,9 @@
 FORWARD = 9
 
 
-def fused_kernel(tab, dest, q, span, pool, out, pages, kv, v_span, v_block, done, done_sem, attn, refs, sems):
+def fused_kernel(
+    dest, slots, flags, q, span, pool, out, pages, over, kv, v_span, v_block, done, done_sem, tab, tab_made, attn, refs, sems
+):
     ex = Exchange(tab, pool, span, pages, kv, refs, sems)
     at = Attention(q, *attn)
     pairs = at.heads // 2
@@ -566,14 +551,22 @@
 
     for quarter in range(QUARTERS):
         ex.pool_own(quarter).start()
+    ex.row[...] = jnp.broadcast_to(jnp.where(flags[...] == 1, slots[...], -1), ex.row.shape)
     ex.barrier()
+    ex.start_rows()
     ex.start_pool()
+    ex.start_new(dest)
+    span_values(span, v_span)
+    at.score_span(0, 0, span[:, :HD])
+    table, most = route(ex.wait_rows())
+    over[0] = jnp.maximum(most, 0)
+    tab_made[...] = table
+    to_scalars = pltpu.make_async_copy(tab_made, tab, sems["table"].at[0])
+    to_scalars.start()
+    to_scalars.wait()
     ex.wait_pool(0)
     ex.pack_y(0)
     ex.pack_y(1)
-    ex.start_new(dest)
-    span_values(span, v_span)
-    at.score_span(0, 0, span[:, :HD])
 
     def write_out(pair):
         cols = pl.ds(pl.multiple_of(pair * 2 * HD, 2 * HD), 2 * HD)
@@ -611,7 +604,7 @@
             def _(b=b):
                 ex.wait_last(2 * b)
                 ex.wait_last(2 * b + 1)
-                block_values(kv[2 * b + 1], tab[9, 0], v_block)
+                block_values(kv[2 * b + 1], tab[0, 9], v_block)
                 at.score(0, 0, kv[2 * b])
 
         @pl.when(step >= first_block)
@@ -635,7 +628,7 @@
 VMEM_MIB = 56
 
 
-def fused(table, dest, queries, span, pool):
+def fused(dest, slots, flags, queries, span, pool):
     refs, sems = exchange_scratch()
     vmem = pl.BlockSpec(memory_space=pltpu.VMEM)
     smem = pl.BlockSpec(memory_space=pltpu.SMEM)
@@ -644,15 +637,21 @@
     rows, width = queries.shape
     return pl.pallas_call(
         fused_kernel,
-        out_shape=[jax.ShapeDtypeStruct((rows, width), bf16), jax.ShapeDtypeStruct((2, PAGE, 2048), bf16)],
-        in_specs=[smem, smem, vmem, vmem, hbm],
-        out_specs=[hbm, hbm],
+        out_shape=[
+            jax.ShapeDtypeStruct((rows, width), bf16),
+            jax.ShapeDtypeStruct((2, PAGE, 2048), bf16),
+            jax.ShapeDtypeStruct((1,), jnp.int32),
+        ],
+        in_specs=[smem, vmem, vmem, vmem, vmem, hbm],
+        out_specs=[hbm, hbm, smem],
         scratch_shapes=[
             pltpu.VMEM((NCH, BLOCK, HD), bf16),
             pltpu.VMEM((HD + ONES, rows), bf16),
             pltpu.VMEM((HD + ONES, BLOCK), bf16),
             pltpu.VMEM((rows, width), bf16),
             pltpu.SemaphoreType.DMA((width // HD // 2,)),
+            pltpu.SMEM((CTXP, 128), jnp.int32),
+            pltpu.VMEM((CTXP, 128), jnp.int32),
             attention_scratch(rows, width),
             refs,
             sems,
@@ -660,10 +659,10 @@
         compiler_params=pltpu.CompilerParams(
             collective_id=1, has_side_effects=True, vmem_limit_bytes=VMEM_MIB * 1024 * 1024
         ),
-    )(table, dest, queries, span, pool)
-
-
-def attend_kernel(tab, q, span, kv, out, v_span, v_block, attn):
+    )(dest, slots, flags, queries, span, pool)
+
+
+def attend_kernel(live, q, span, kv, out, v_span, v_block, attn):
     at = Attention(q, *attn)
     pairs = at.heads // 2
     span_values(span, v_span)
@@ -675,7 +674,7 @@
 
     @pl.loop(0, QUARTERS)
     def _(b):
-        block_values(kv[2 * b + 1], tab[9, 0], v_block)
+        block_values(kv[2 * b + 1], live[0], v_block)
         at.score(0, 0, kv[2 * b])
 
         @pl.loop(0, pairs)
@@ -687,7 +686,7 @@
         out[:, at.columns(n)] = at.result(n)
 
 
-def attend(table, queries, span, kv):
+def attend(live, queries, span, kv):
     rows, width = queries.shape
     vmem = pl.BlockSpec(memory_space=pltpu.VMEM)
     smem = pl.BlockSpec(memory_space=pltpu.SMEM)
@@ -702,10 +701,10 @@
             attention_scratch(rows, width),
         ],
         compiler_params=pltpu.CompilerParams(vmem_limit_bytes=48 * 1024 * 1024),
-    )(table, queries, span, kv)
-
-
-def dense(table, dest, queries, span, pool, slots, flags):
+    )(live, queries, span, kv)
+
+
+def dense(dest, queries, span, pool, slots, flags):
     tp_size, dec_size = lax.axis_size("tp"), lax.axis_size("dec")
     devices = tp_size * dec_size
     width = span.shape[1]
@@ -724,16 +723,17 @@
     outgoing = jnp.einsum("dp,pkc->dkc", chosen, new_pages, preferred_element_type=jnp.float32).astype(jnp.bfloat16)
     placed = lax.all_to_all(outgoing, "dec", split_axis=0, concat_axis=0, tiled=True)
     placed = lax.all_to_all(placed, "tp", split_axis=0, concat_axis=2, tiled=True)
-    return (attend(table, queries, span, cached), placed)
+    return (attend(live_count.reshape(1), queries, span, cached), placed)
 
 
 def body(queries, span_kv, page_pool, cache_slot, cache_live, span_dest):
-    table = make_table(cache_slot, cache_live)
+    dest, q, span = span_dest[0], queries[0], span_kv[0]
+    attn_out, placed, over = fused(dest, cache_slot.reshape(1, -1), cache_live.reshape(1, -1), q, span, page_pool)
     attn_out, placed = lax.cond(
-        table[10, 0] > 0,
-        lambda *a: dense(*a),
-        lambda tab, dest, q, span, pool, slots, flags: tuple(fused(tab, dest, q, span, pool)),
-        table, span_dest[0], queries[0], span_kv[0], page_pool, cache_slot[0], cache_live[0],
+        over[0] > 0,
+        lambda attn, pages, *a: dense(*a),
+        lambda attn, pages, *a: (attn, pages),
+        attn_out, placed, dest, q, span, page_pool, cache_slot[0], cache_live[0],
     )
     return (attn_out[None], placed)
 

time: 101 us -> 100 us (0.990)
  local copies, waits for them, and re-layouts: 3.22 us -> 2.13 us
    pallas_call x1, Pallas kernels: 85.5 us -> 96.6 us  [fused(): pl.pallas_call(fused_kernel, out_shape=[jax.ShapeDtypeStruct((rows, width...]
    pallas_call x1 -> x0, Pallas kernels: 10.3 us -> none  [make_table(): pl.pallas_call(table_kernel, out_shape=jax.ShapeDtypeStruct((LISTS, 128),...]
    unnamed x2 -> x10, local copies, waits for them, and re-layouts: 2.11 us -> 2.13 us
where the time goes in v6:
time: 100 us
  Pallas kernels  96.6 us (97%)
  local copies, waits for them, and re-layouts  2.13 us (2%)
  between operations  1.32 us (1%)
    pallas_call x1, Pallas kernels, fused(): pl.pallas_call(fused_kernel, out_shape=[jax.ShapeDtypeStruct((rows, width...  96.6 us
    unnamed x10, local copies, waits for them, and re-layouts  2.13 us

profile of v6, /device:TPU:1, one launch (start us, length us, event | category | flops | bytes accessed | tf_op | source)
XLA Modules:
  0.0 100.1 jit_solution(10783759936335829947)
XLA Ops:
  0.6 0.0 copy-start.1
  0.6 0.0 copy-start.2
  0.7 0.0 copy-start.3
  0.7 0.0 copy-start.4
  0.7 96.6 %shard_map.77 = (bf16[768,1024]{1,0:T(8,128)(2,1)S(1)}, bf16[2,128,2048]{2,1,0:T(8,128)(2,1)S(1)}, s32[1]{0:T(128)}) custom-call(s32[6]{0:T(128)} %bitcast.56, s32[1,128]{1,0:T(1,128)} %bitcast.58, s32[1,128]{1,0:T(1,128)} %bitcast.60, bf16[768,1024]{1,0:T(8,128)(2,1)} %bitcast.46, bf16[768,256]{1,0:T(8,128)(2,1)} %bitcast.48, bf16[8,128,2048]{2,1,0:T(8,128)(2,1)} %pool.1), custom_call_target="tpu_custom_call" | custom-call | tf_op jit(solution)/shard_map/pallas_call | solution.py:638
  97.9 0.0 copy-done.1
  97.9 0.0 copy-done.2
  97.9 0.0 copy-done.3
  97.9 0.0 copy-done.4
  97.9 1.1 %copy.74 = bf16[1,768,1024]{2,1,0:T(8,128)(2,1)} copy(bf16[1,768,1024]{2,1,0:T(8,128)(2,1)S(1)} %get-tuple-element.89) | data formatting | bytes 3145728
  99.1 1.0 copy.75
  (1 shorter events, 0.0 us)
Async XLA Ops:
  0.6 97.3 %copy-start.1 = (bf16[1,768,256]{2,1,0:T(8,128)(2,1)S(1)}, bf16[1,768,256]{2,1,0:T(8,128)(2,1)}, u32[]{:S(2)}) copy-start(bf16[1,768,256]{2,1,0:T(8,128)(2,1)} %param.9) | copy-start | bytes 1179652
  0.6 97.3 %copy-start.2 = (s32[1,6]{1,0:T(1,128)S(1)}, s32[1,6]{1,0:T(1,128)}, u32[]{:S(2)}) copy-start(s32[1,6]{1,0:T(1,128)} %param.13) | copy-start | bytes 76
  0.7 97.3 %copy-start.3 = (s32[1,128,1]{1,2,0:T(1,128)S(1)}, s32[1,128,1]{1,2,0:T(1,128)}, u32[]{:S(2)}) copy-start(s32[1,128,1]{1,2,0:T(1,128)} %param.11) | copy-start | bytes 1540
  0.7 97.3 %copy-start.4 = (s32[1,128,1]{1,2,0:T(1,128)S(1)}, s32[1,128,1]{1,2,0:T(1,128)}, u32[]{:S(2)}) copy-start(s32[1,128,1]{1,2,0:T(1,128)} %param.12) | copy-start | bytes 1540

commit v7 on v6

--- a/solution.py
+++ b/solution.py
@@ -122,7 +122,8 @@
         size = jnp.sum(flag(live & (g == (d // 2) * 2 + c))).astype(jnp.int32)
         table = jnp.where((lane == 7 + c) & (place >= size), table[0:1, :], table)
     table = jnp.where(lane == 9, held, table)
-    return table, over
+    sizes = jnp.where(lane < 1, 16, jnp.where(lane < 3, 4 * CAP_Y, jnp.where(lane < 7, 4 * CAP_Z, 4 * CAP_X)))
+    return jnp.minimum(jnp.maximum(table, 0), sizes - 1), over
 
 
 QUARTERS = 4
@@ -159,8 +160,8 @@
 
         pl.semaphore_wait(sem, 41 - jnp.where(t % 2 == zlo, 1, 0))
 
-    def entry(self, place, column, size):
-        return jnp.minimum(jnp.maximum(self.tab[place, column], 0), size - 1)
+    def entry(self, place, column):
+        return self.tab[place, column]
 
     def peer(self, axis, k):
         t, d, y, z, x, c = self.t, self.d, self.y, self.z, self.x, self.core
@@ -249,7 +250,7 @@
 
         @pl.loop(0, CAP_Y, unroll=True)
         def _(n):
-            slot = self.entry(n, 0, 16)
+            slot = self.entry(n, 0)
             for k in range(4):
                 to = (self.y + k) % 4
                 for zhi in range(2):
@@ -269,7 +270,7 @@
         def _(n):
             for k in range(4):
                 to = (self.z + k) % 4
-                block = self.recv_y[ch][self.entry(n, 1 + to % 2, 4 * CAP_Y) * 2 + to // 2]
+                block = self.recv_y[ch][self.entry(n, 1 + to % 2) * 2 + to // 2]
                 if k == 0:
                     self.recv_z[ch][self.z * CAP_Z + n] = block
                 else:
@@ -284,7 +285,7 @@
         def _(n):
             for k in range(4):
                 to = (self.x + k) % 4
-                block = self.recv_z[ch][self.entry(n, 3 + to, 4 * CAP_Z)]
+                block = self.recv_z[ch][self.entry(n, 3 + to)]
                 if k == 0:
                     self.recv_x[ch][self.x * CAP_X + n] = block
                 else:
@@ -308,8 +309,8 @@
         def _(n):
             rows = pl.ds(pl.multiple_of(n * ROWS, ROWS), ROWS)
             own = pl.ds(pl.multiple_of((self.core * CTXP + n) * ROWS, ROWS), ROWS)
-            self.kv[ch, own, :] = self.recv_x[ch][self.entry(n, 7 + self.core, 4 * CAP_X)]
-            self.send_c[ch, rows, :] = self.recv_x[ch][self.entry(n, 8 - self.core, 4 * CAP_X)]
+            self.kv[ch, own, :] = self.recv_x[ch][self.entry(n, 7 + self.core)]
+            self.send_c[ch, rows, :] = self.recv_x[ch][self.entry(n, 8 - self.core)]
 
         self.last(ch, self.core).start()
 

time: 100 us -> 99.1 us (level)
  Pallas kernels: 96.6 us -> 95.2 us
    pallas_call x1, Pallas kernels: 96.6 us -> 95.2 us  [fused(): pl.pallas_call(fused_kernel, out_shape=[jax.ShapeDtypeStruct((rows, width...]
where the time goes in v7:
time: 99.1 us; the launch traced here: 98.8 us
  Pallas kernels  95.2 us (96%)
  local copies, waits for them, and re-layouts  2.13 us (2%)
  between operations  1.32 us (1%)
    pallas_call x1, Pallas kernels, fused(): pl.pallas_call(fused_kernel, out_shape=[jax.ShapeDtypeStruct((rows, width...  95.2 us
    unnamed x10, local copies, waits for them, and re-layouts  2.13 us

profile of v7, /device:TPU:1, one launch (start us, length us, event | category | flops | bytes accessed | tf_op | source)
XLA Modules:
  0.0 98.8 jit_solution(4311641533405918061)
XLA Ops:
  0.6 0.0 copy-start.1
  0.6 0.0 copy-start.2
  0.7 0.0 copy-start.3
  0.7 0.0 copy-start.4
  0.7 95.2 %shard_map.77 = (bf16[768,1024]{1,0:T(8,128)(2,1)S(1)}, bf16[2,128,2048]{2,1,0:T(8,128)(2,1)S(1)}, s32[1]{0:T(128)}) custom-call(s32[6]{0:T(128)} %bitcast.56, s32[1,128]{1,0:T(1,128)} %bitcast.58, s32[1,128]{1,0:T(1,128)} %bitcast.60, bf16[768,1024]{1,0:T(8,128)(2,1)} %bitcast.46, bf16[768,256]{1,0:T(8,128)(2,1)} %bitcast.48, bf16[8,128,2048]{2,1,0:T(8,128)(2,1)} %pool.1), custom_call_target="tpu_custom_call" | custom-call | tf_op jit(solution)/shard_map/pallas_call | solution.py:639
  96.4 0.0 copy-done.1
  96.5 0.0 copy-done.2
  96.5 0.0 copy-done.3
  96.5 0.0 copy-done.4
  96.5 0.2 conditional.1
  96.7 1.1 %copy.74 = bf16[1,768,1024]{2,1,0:T(8,128)(2,1)} copy(bf16[1,768,1024]{2,1,0:T(8,128)(2,1)S(1)} %get-tuple-element.89) | data formatting | bytes 3145728
  97.9 1.0 copy.75
Async XLA Ops:
  0.6 95.8 %copy-start.1 = (bf16[1,768,256]{2,1,0:T(8,128)(2,1)S(1)}, bf16[1,768,256]{2,1,0:T(8,128)(2,1)}, u32[]{:S(2)}) copy-start(bf16[1,768,256]{2,1,0:T(8,128)(2,1)} %param.9) | copy-start | bytes 1179652
  0.6 95.8 %copy-start.2 = (s32[1,6]{1,0:T(1,128)S(1)}, s32[1,6]{1,0:T(1,128)}, u32[]{:S(2)}) copy-start(s32[1,6]{1,0:T(1,128)} %param.13) | copy-start | bytes 76
  0.7 95.8 %copy-start.3 = (s32[1,128,1]{1,2,0:T(1,128)S(1)}, s32[1,128,1]{1,2,0:T(1,128)}, u32[]{:S(2)}) copy-start(s32[1,128,1]{1,2,0:T(1,128)} %param.11) | copy-start | bytes 1540
  0.7 95.8 %copy-start.4 = (s32[1,128,1]{1,2,0:T(1,128)S(1)}, s32[1,128,1]{1,2,0:T(1,128)}, u32[]{:S(2)}) copy-start(s32[1,128,1]{1,2,0:T(1,128)} %param.12) | copy-start | bytes 1540

commit v8 on v7

--- a/solution.py
+++ b/solution.py
@@ -197,7 +197,7 @@
     def wait_rows(self):
         for k in range(1, 16):
             self.row_copy(k, (self.d + 16 - k) % 16).wait_recv()
-        return jnp.concatenate([self.rows[g, 0:1, :] for g in range(16)], axis=0)
+        return jnp.concatenate([self.rows[g] for g in range(16)], axis=0)
 
     def pool_own(self, half):
         rows = pl.ds(self.core * 64 + half * ROWS, ROWS)
@@ -420,8 +420,8 @@
         vmem((7, PAGE, 256), bf16),
         vmem((3, 4, PAGE, 256), bf16),
         vmem((4, 4, PAGE, 256), bf16),
-        vmem((8, 128), jnp.int32),
-        vmem((16, 8, 128), jnp.int32),
+        vmem((1, 128), jnp.int32),
+        vmem((16, 1, 128), jnp.int32),
     ]
     sems = {
         "own": dma((QUARTERS,)), "pair_send": dma((QUARTERS,)), "pair_recv": dma((QUARTERS,)), "send": dma((3, NCH, 3)),
@@ -552,7 +552,7 @@
 
     for quarter in range(QUARTERS):
         ex.pool_own(quarter).start()
-    ex.row[...] = jnp.broadcast_to(jnp.where(flags[...] == 1, slots[...], -1), ex.row.shape)
+    ex.row[...] = jnp.where(flags[...] == 1, slots[...], -1)
     ex.barrier()
     ex.start_rows()
     ex.start_pool()
@@ -603,6 +603,8 @@
 
             @pl.when(step == first_block + b * pairs)
             def _(b=b):
+                if b == QUARTERS - 1:
+                    ex.wait_sends()
                 ex.wait_last(2 * b)
                 ex.wait_last(2 * b + 1)
                 block_values(kv[2 * b + 1], tab[0, 9], v_block)
@@ -623,7 +625,6 @@
     for pair in range(pairs):
         write_out(pair).wait()
     ex.wait_new()
-    ex.wait_sends()
 
 
 VMEM_MIB = 56

time: 99.1 us -> 107 us (1.080)
  Pallas kernels: 95.2 us -> 103 us
    pallas_call x1, Pallas kernels: 95.2 us -> 103 us  [fused(): pl.pallas_call(fused_kernel, out_shape=[jax.ShapeDtypeStruct((rows, width...]
where the time goes in v8:
time: 107 us
  Pallas kernels  103 us (96%)
  local copies, waits for them, and re-layouts  2.13 us (2%)
  between operations  1.32 us (1%)
    pallas_call x1, Pallas kernels, fused(): pl.pallas_call(fused_kernel, out_shape=[jax.ShapeDtypeStruct((rows, width...  103 us

profile of v8, /device:TPU:1, one launch (start us, length us, event | category | flops | bytes accessed | tf_op | source)
XLA Modules:
  0.0 106.7 jit_solution(10504427565032064655)
XLA Ops:
  0.6 0.0 copy-start.1
  0.6 0.0 copy-start.2
  0.7 0.0 copy-start.3
  0.7 0.0 copy-start.4
  0.7 103.1 %shard_map.77 = (bf16[768,1024]{1,0:T(8,128)(2,1)S(1)}, bf16[2,128,2048]{2,1,0:T(8,128)(2,1)S(1)}, s32[1]{0:T(128)}) custom-call(s32[6]{0:T(128)} %bitcast.56, s32[1,128]{1,0:T(1,128)} %bitcast.58, s32[1,128]{1,0:T(1,128)} %bitcast.60, bf16[768,1024]{1,0:T(8,128)(2,1)} %bitcast.46, bf16[768,256]{1,0:T(8,128)(2,1)} %bitcast.48, bf16[8,128,2048]{2,1,0:T(8,128)(2,1)} %pool.1), custom_call_target="tpu_custom_call" | custom-call | tf_op jit(solution)/shard_map/pallas_call | solution.py:640
  104.3 0.0 copy-done.1
  104.4 0.0 copy-done.2
  104.4 0.0 copy-done.3
  104.4 0.0 copy-done.4
  104.4 0.2 conditional.1
  104.6 1.1 %copy.74 = bf16[1,768,1024]{2,1,0:T(8,128)(2,1)} copy(bf16[1,768,1024]{2,1,0:T(8,128)(2,1)S(1)} %get-tuple-element.89) | data formatting | bytes 3145728
  105.8 1.0 copy.75
Async XLA Ops:
  0.6 103.7 %copy-start.1 = (bf16[1,768,256]{2,1,0:T(8,128)(2,1)S(1)}, bf16[1,768,256]{2,1,0:T(8,128)(2,1)}, u32[]{:S(2)}) copy-start(bf16[1,768,256]{2,1,0:T(8,128)(2,1)} %param.9) | copy-start | bytes 1179652
  0.6 103.7 %copy-start.2 = (s32[1,6]{1,0:T(1,128)S(1)}, s32[1,6]{1,0:T(1,128)}, u32[]{:S(2)}) copy-start(s32[1,6]{1,0:T(1,128)} %param.13) | copy-start | bytes 76
  0.7 103.7 %copy-start.3 = (s32[1,128,1]{1,2,0:T(1,128)S(1)}, s32[1,128,1]{1,2,0:T(1,128)}, u32[]{:S(2)}) copy-start(s32[1,128,1]{1,2,0:T(1,128)} %param.11) | copy-start | bytes 1540
  0.7 103.7 %copy-start.4 = (s32[1,128,1]{1,2,0:T(1,128)S(1)}, s32[1,128,1]{1,2,0:T(1,128)}, u32[]{:S(2)}) copy-start(s32[1,128,1]{1,2,0:T(1,128)} %param.12) | copy-start | bytes 1540
